TPU v7x, 512 devices: a whole 4x4x16 slice. The times are simulated.
512 devices in a mesh: ctx: 128 (over y, z, x_lo), tp: 4 (over x_hi, core).
Axes of the slice: x: 4 (x_hi: 2, x_lo: 2; x = x_hi * 2 + x_lo), y: 4, z: 16, core: 2. Of those that a mesh axis runs over, the one named last changes fastest.
Arguments:
- streams: bfloat16 [3, 16384, 1024], P(None, 'ctx', 'tp'), may hold values from -6 to 6
- short_taps: float32 [3, 3, 1024], P(None, None, 'tp'), may hold values from -4 to 4
- w_first: float32 [33, 64], replicated, may hold values from -4 to 4
- b_first: float32 [64], replicated, may hold values from -3.140625 to 3.140625
- w_second: float32 [64, 64], replicated, may hold values from -0.75 to 0.75
- b_second: float32 [64], replicated, may hold values from -3.140625 to 3.140625
- w_last: float32 [64, 1024], P(None, 'tp'), may hold values from -0.75 to 0.75
- decay_rate: float32 [1024], P('tp'), may hold values from 1.5258789e-05 to 0.03
- skip_gain: float32 [1024], P('tp'), may hold values from 0.5 to 1.5
- cotangent: bfloat16 [16384, 1024], P('ctx', 'tp'), may hold values from -19 to 19
Outputs:
- output: bfloat16 [16384, 1024], P('ctx', 'tp')
- grad_streams: bfloat16 [3, 16384, 1024], P(None, 'ctx', 'tp')
- grad_taps: float32 [3, 3, 1024], P(None, None, 'tp')
- grad_w_first: float32 [33, 64], replicated
- grad_b_first: float32 [64], replicated
- grad_w_second: float32 [64, 64], replicated
- grad_b_second: float32 [64], replicated
- grad_w_last: float32 [64, 1024], P(None, 'tp')
- grad_rate: float32 [1024], P('tp')
- grad_skip: float32 [1024], P('tp')
All inputs are finite; a program needn't handle non-finite values.
Results may differ from a plain program's by a relative error of at most 0.012.
Values may be sent and summed in bfloat16 or wider, within the bound.
No kernel may reach another device: no remote copies, remote signals or barrier semaphores. Data moves between devices by JAX's collectives and lax.ppermute only.
A program may use at most 128 MiB of HBM per device.

v0:
```python
import math

import jax
import jax.numpy as jnp
from jax import lax
from jax.sharding import PartitionSpec as P

exact_prec = lax.Precision.HIGHEST


def passed_along(block, axis, distance):
    devices = range(lax.axis_size(axis))
    route = [(i - distance, i) for i in devices if i - distance in devices]
    return lax.ppermute(block, axis, route)


def features_at(positions, seq_len, band_count):
    frequency = jnp.arange(1, band_count + 1, dtype=jnp.int32)
    phases = frequency[:, None] * positions[None, :] % seq_len
    angles = 2.0 * math.pi / seq_len * phases.astype(jnp.float32)
    linear = positions.astype(jnp.float32)[None, :] / seq_len
    return jnp.concatenate([linear, jnp.cos(angles), jnp.sin(angles)], axis=0)


def filter_forward(
    positions, seq_len, band_count, w_first, b_first, w_second, b_second, w_cols, rates
):
    feat = features_at(positions, seq_len, band_count)
    pre_one = jnp.dot(w_first.T, feat, precision=exact_prec) + b_first[:, None]
    pre_two = jnp.dot(w_second.T, jnp.sin(pre_one), precision=exact_prec) + b_second[:, None]
    raw_filter = jnp.dot(w_cols.T, jnp.sin(pre_two), precision=exact_prec)
    window = jnp.sqrt(2.0 * rates)[:, None] * jnp.exp(
        -rates[:, None] * positions.astype(jnp.float32)[None, :]
    )
    return (feat, pre_one, pre_two, raw_filter, window)


def filter_backward(saved, w_second, w_cols, rates, positions, grad_filt):
    feat, pre_one, pre_two, raw_filter, window = saved
    grad_raw = grad_filt * window
    grad_rate = jnp.sum(
        grad_filt
        * raw_filter
        * window
        * (0.5 / rates[:, None] - positions.astype(jnp.float32)[None, :]),
        axis=1,
    )
    grad_w_last = jnp.dot(jnp.sin(pre_two), grad_raw.T, precision=exact_prec)
    grad_pre_two = jnp.dot(w_cols, grad_raw, precision=exact_prec) * jnp.cos(pre_two)
    grad_w_second = jnp.dot(jnp.sin(pre_one), grad_pre_two.T, precision=exact_prec)
    grad_b_second = jnp.sum(grad_pre_two, axis=1)
    grad_pre_one = jnp.dot(w_second, grad_pre_two, precision=exact_prec) * jnp.cos(pre_one)
    grad_w_first = jnp.dot(feat, grad_pre_one.T, precision=exact_prec)
    grad_b_first = jnp.sum(grad_pre_one, axis=1)
    return (grad_w_last, grad_rate, grad_w_first, grad_b_first, grad_w_second, grad_b_second)


def table_pair(count):
    indices = jnp.arange(count, dtype=jnp.int32)
    angles = (
        2.0 * math.pi / count * (indices[:, None] * indices[None, :] % count).astype(jnp.float32)
    )
    return (jnp.cos(angles), jnp.sin(angles))


def dft_tables(rows_count, cols_count):
    cos_rows, sin_rows = table_pair(rows_count)
    cos_cols, sin_cols = table_pair(cols_count)
    total = rows_count * cols_count
    row_index = jnp.arange(rows_count, dtype=jnp.int32)
    col_index = jnp.arange(cols_count, dtype=jnp.int32)
    angles = (
        2.0
        * math.pi
        / total
        * (row_index[:, None] * col_index[None, :] % total).astype(jnp.float32)
    )
    return (cos_rows, sin_rows, cos_cols, sin_cols, jnp.cos(angles), jnp.sin(angles))


def forward_dft(signal, tables):
    cos_rows, sin_rows, cos_cols, sin_cols, twist_cos, twist_sin = tables
    half_rows = signal.shape[1]
    inner_real = jnp.einsum("kn,cnb->ckb", cos_rows[:, :half_rows], signal, precision=exact_prec)
    inner_imag = -jnp.einsum("kn,cnb->ckb", sin_rows[:, :half_rows], signal, precision=exact_prec)
    turned_real = inner_real * twist_cos + inner_imag * twist_sin
    turned_imag = inner_imag * twist_cos - inner_real * twist_sin
    outer_real = jnp.einsum(
        "ckb,bj->ckj", turned_real, cos_cols, precision=exact_prec
    ) + jnp.einsum("ckb,bj->ckj", turned_imag, sin_cols, precision=exact_prec)
    outer_imag = jnp.einsum(
        "ckb,bj->ckj", turned_imag, cos_cols, precision=exact_prec
    ) - jnp.einsum("ckb,bj->ckj", turned_real, sin_cols, precision=exact_prec)
    return (outer_real, outer_imag)


def inverse_dft(spec_real, spec_imag, half_rows, tables):
    cos_rows, sin_rows, cos_cols, sin_cols, twist_cos, twist_sin = tables
    total = cos_rows.shape[0] * cos_cols.shape[0]
    inner_real = jnp.einsum("ckj,jb->ckb", spec_real, cos_cols, precision=exact_prec) - jnp.einsum(
        "ckj,jb->ckb", spec_imag, sin_cols, precision=exact_prec
    )
    inner_imag = jnp.einsum("ckj,jb->ckb", spec_imag, cos_cols, precision=exact_prec) + jnp.einsum(
        "ckj,jb->ckb", spec_real, sin_cols, precision=exact_prec
    )
    turned_real = inner_real * twist_cos - inner_imag * twist_sin
    turned_imag = inner_imag * twist_cos + inner_real * twist_sin
    result = jnp.einsum(
        "nk,ckb->cnb", cos_rows[:half_rows], turned_real, precision=exact_prec
    ) - jnp.einsum("nk,ckb->cnb", sin_rows[:half_rows], turned_imag, precision=exact_prec)
    return result / total


def times_spec(left, right, conjugate_left):
    left_real, left_imag = left
    right_real, right_imag = right
    if conjugate_left:
        left_imag = -left_imag
    return (
        left_real * right_real - left_imag * right_imag,
        left_real * right_imag + left_imag * right_real,
    )


def backward_spectra(
    owner_grad, gated_spec, filt_spec, own_skip, own_count, ctx_count, tok_rows, tables
):
    seq_len = ctx_count * tok_rows
    grad_spec = forward_dft(owner_grad.reshape(own_count, ctx_count, tok_rows), tables)
    back_gated = times_spec(filt_spec, grad_spec, True)
    owner_grad_gated = (
        inverse_dft(back_gated[0], back_gated[1], ctx_count, tables).reshape(own_count, seq_len)
        + own_skip[:, None] * owner_grad
    ).astype(jnp.bfloat16)
    back_filt = times_spec(gated_spec, grad_spec, True)
    owner_grad_filt = (
        inverse_dft(back_filt[0], back_filt[1], ctx_count, tables)
        .reshape(own_count, seq_len)
        .astype(jnp.bfloat16)
    )
    return (owner_grad_gated, owner_grad_filt)


def on_device(
    streams,
    short_taps,
    w_first,
    b_first,
    w_second,
    b_second,
    w_last,
    decay_rate,
    skip_gain,
    cotangent,
):
    ctx_count = lax.axis_size("ctx")
    ctx_rank = lax.axis_index("ctx")
    tok_rows = streams.shape[1]
    channels = streams.shape[2]
    seq_len = tok_rows * ctx_count
    own_count = channels // ctx_count
    band_count = (w_first.shape[0] - 1) // 2
    row_positions = ctx_rank * tok_rows + jnp.arange(tok_rows, dtype=jnp.int32)
    signal = streams.astype(jnp.float32)
    history = passed_along(streams[:, tok_rows - 2 :, :], "ctx", 1)
    padded = jnp.concatenate([history.astype(jnp.float32), signal], axis=1)
    tap_list = [short_taps[:, offset][:, None, :] for offset in range(3)]
    side = (
        tap_list[0] * padded[:, 2:] + tap_list[1] * padded[:, 1:-1] + tap_list[2] * padded[:, :-2]
    )
    query_side, key_side, value_side = (side[0], side[1], side[2])
    gated = (key_side * value_side).astype(jnp.bfloat16)
    grad_out = cotangent.astype(jnp.float32)
    grad_mixed = (grad_out * query_side).astype(jnp.bfloat16)
    own_skip = lax.dynamic_slice_in_dim(skip_gain, ctx_rank * own_count, own_count, 0)
    saved = filter_forward(
        row_positions, seq_len, band_count, w_first, b_first, w_second, b_second, w_last, decay_rate
    )
    row_filt = (saved[3] * saved[4]).astype(jnp.bfloat16).T
    received, filt_received = (
        lax.all_to_all(gated, "ctx", split_axis=1, concat_axis=0, tiled=True),
        lax.all_to_all(row_filt, "ctx", split_axis=1, concat_axis=0, tiled=True),
    )
    owner_filt = filt_received.T
    tables = dft_tables(2 * ctx_count, tok_rows)
    owner_gated = received.T.astype(jnp.float32)
    gated_spec = forward_dft(owner_gated.reshape(own_count, ctx_count, tok_rows), tables)
    filt_spec = forward_dft(
        owner_filt.astype(jnp.float32).reshape(own_count, ctx_count, tok_rows), tables
    )
    product = times_spec(gated_spec, filt_spec, False)
    long_conv = inverse_dft(product[0], product[1], ctx_count, tables).reshape(own_count, seq_len)
    owner_mixed = (long_conv + own_skip[:, None] * owner_gated).astype(jnp.bfloat16)
    mixed = lax.all_to_all(owner_mixed.T, "ctx", split_axis=0, concat_axis=1, tiled=True)
    owner_grad = lax.all_to_all(
        grad_mixed, "ctx", split_axis=1, concat_axis=0, tiled=True
    ).T.astype(jnp.float32)
    owner_grad_gated, owner_grad_filt = backward_spectra(
        owner_grad, gated_spec, filt_spec, own_skip, own_count, ctx_count, tok_rows, tables
    )
    grad_gated, row_grad_filt = (
        lax.all_to_all(owner_grad_gated.T, "ctx", split_axis=0, concat_axis=1, tiled=True),
        lax.all_to_all(owner_grad_filt.T, "ctx", split_axis=0, concat_axis=1, tiled=True),
    )
    filter_grads = filter_backward(
        saved, w_second, w_last, decay_rate, row_positions, row_grad_filt.T.astype(jnp.float32)
    )
    mixed_full = mixed.astype(jnp.float32)
    output = (query_side * mixed_full).astype(jnp.bfloat16)
    grad_skip_part = jnp.sum(grad_mixed.astype(jnp.float32) * gated.astype(jnp.float32), axis=0)
    grad_gated_full = grad_gated.astype(jnp.float32)
    grad_side = jnp.stack(
        [grad_out * mixed_full, grad_gated_full * value_side, grad_gated_full * key_side]
    )
    ahead = passed_along(grad_side[:, :2, :], "ctx", -1)
    grad_pad = jnp.concatenate([grad_side, ahead], axis=1)
    grad_streams = (
        tap_list[0] * grad_pad[:, :tok_rows]
        + tap_list[1] * grad_pad[:, 1 : tok_rows + 1]
        + tap_list[2] * grad_pad[:, 2:]
    ).astype(jnp.bfloat16)
    taps_part = jnp.stack(
        [
            jnp.sum(grad_side * padded[:, 2 - offset : 2 - offset + tok_rows], axis=1)
            for offset in range(3)
        ],
        axis=1,
    )
    last_part, rate_part, first_part, first_bias, second_part, second_bias = filter_grads
    grad_taps, grad_skip, grad_w_last, grad_rate = lax.psum(
        (taps_part, grad_skip_part, last_part, rate_part), "ctx"
    )
    grad_w_first, grad_b_first, grad_w_second, grad_b_second = lax.psum(
        (first_part, first_bias, second_part, second_bias), ("ctx", "tp")
    )
    return (
        output,
        grad_streams,
        grad_taps,
        grad_w_first,
        grad_b_first,
        grad_w_second,
        grad_b_second,
        grad_w_last,
        grad_rate,
        grad_skip,
    )


def solution(mesh):
    return jax.shard_map(
        on_device,
        mesh=mesh,
        in_specs=(
            P(None, "ctx", "tp"),
            P(None, None, "tp"),
            P(),
            P(),
            P(),
            P(),
            P(None, "tp"),
            P("tp"),
            P("tp"),
            P("ctx", "tp"),
        ),
        out_specs=(
            P("ctx", "tp"),
            P(None, "ctx", "tp"),
            P(None, None, "tp"),
            P(),
            P(),
            P(),
            P(),
            P(None, "tp"),
            P("tp"),
            P("tp"),
        ),
        check_vma=False,
    )
```

profile of v0, /device:TPU:2, one launch (start us, length us, event | category | flops | bytes accessed | tf_op | source)
XLA Modules:
  0.0 1190.1 jit_solution(6991175883219081596)
XLA Ops:
  10.1 1.0 multiply_convert_fusion.1
  11.8 20.5 %all-to-all-start.1 = ((bf16[128,128,2]{0,2,1:T(2,128)(2,1)}), bf16[128,128,2]{0,2,1:T(2,128)(2,1)S(1)}, u32[]{:S(2)}, u32[]{:S(2)}) async-start(bf16[128,128,2]{0,2,1:T(2,128)(2,1)} %bitcast.11), calls=%async_computation.1 | async-start | bytes 131072 | tf_op jit(solution)/shard_map/all_to_all | solution.py:182
  32.5 3.4 collective-permute-start
  36.9 1.0 fusion.66
  42.3 4.9 all-to-all-done.1
  47.2 13.6 %all-to-all-start = ((bf16[128,128,2]{0,2,1:T(2,128)(2,1)}), bf16[128,128,2]{0,2,1:T(2,128)(2,1)S(1)}, u32[]{:S(2)}, u32[]{:S(2)}) async-start(bf16[128,128,2]{0,2,1:T(2,128)(2,1)} %bitcast.1), calls=%async_computation | async-start | bytes 131072 | tf_op jit(solution)/shard_map/all_to_all | solution.py:181
  62.3 1.5 convolution_add_fusion.4
  64.5 1.5 convolution_subtract_fusion.4
  66.0 9.8 all-to-all-done
  75.7 7.6 all-to-all-start.3
  84.0 14.1 %all-to-all-done.3 = bf16[128,128,2]{0,2,1:T(2,128)(2,1)S(1)} async-done(((bf16[128,128,2]{0,2,1:T(2,128)(2,1)}), bf16[128,128,2]{0,2,1:T(2,128)(2,1)S(1)}, u32[]{:S(2)}, u32[]{:S(2)}) %all-to-all-start.3) | async-done | bytes 65568 | tf_op jit(solution)/shard_map/all_to_all | solution.py:195
  104.7 1.5 multiply_subtract_fusion
  110.4 7.6 all-to-all-start.5
  127.1 5.6 all-to-all-done.5
  132.8 11.6 all-to-all-start.4
  147.9 11.3 all-to-all-done.4
  159.2 6.9 all-to-all-start.2
  166.4 14.7 %all-to-all-done.2 = bf16[128,128,2]{1,2,0:T(2,128)(2,1)S(1)} async-done(((bf16[128,128,2]{1,2,0:T(2,128)(2,1)}), bf16[128,128,2]{1,2,0:T(2,128)(2,1)S(1)}, u32[]{:S(2)}, u32[]{:S(2)}) %all-to-all-start.2) | async-done | bytes 65568 | tf_op jit(solution)/shard_map/all_to_all | solution.py:194
  181.2 3.3 collective-permute-start.1
  185.5 99.0 %all-reduce = (f32[33,64]{1,0:T(8,128)}, f32[64]{0:T(128)}, f32[64,64]{1,0:T(8,128)}, f32[64]{0:T(128)}) all-reduce(f32[33,64]{1,0:T(8,128)S(1)} %fusion.160, f32[64]{0:T(128)S(1)} %get-tuple-element.74, f32[64,64]{1,0:T(8,128)S(1)} %fusion.271, f32[64]{0:T(128)S(1)} %get-tuple-element.76), channel_id=1, replica_groups=mesh['ctx'=128,'tp'=4] {'ctx','tp'}, use_global_device_ids=true, to_apply=%region_4.5 | all-reduce | flops 6336 | bytes 50688 | tf_op jit(solution)/shard_map/psum | solution.py:233
  284.5 1.3 multiply_reduce_fusion.1
  285.8 603.7 %all-reduce.1 = (f32[3,3,256]{2,0,1:T(4,128)S(1)}, f32[256]{0:T(256)}, f32[256]{0:T(256)}) all-reduce(f32[3,3,256]{2,0,1:T(4,128)S(1)} %pad_maximum_fusion.6, f32[256]{0:T(256)S(1)} %fusion.51, f32[256]{0:T(256)S(1)} %get-tuple-element.40), channel_id=1, replica_groups=mesh['ctx'=128,'tp'=4] {'ctx'}, use_global_device_ids=true, to_apply=%region_3.4 | all-reduce | flops 2816 | bytes 22528 | tf_op jit(solution)/shard_map/psum | solution.py:230
  890.9 290.7 %all-reduce.4.cloned.1.call-done = f32[64,256]{1,0:T(8,128)} async-done(((f32[64,256]{1,0:T(8,128)}), f32[64,256]{1,0:T(8,128)}) %all-reduce.4.cloned.1.call-update) | async-done | bytes 65552 | tf_op jit(solution)/shard_map/psum | solution.py:230
  1181.5 1.5 copy.208
  (126 shorter events, 37.7 us)
Async XLA Ops:
  7.2 2.9 copy-start
  7.2 0.8 copy-start.19
  10.1 1.0 copy-start.11
  11.1 21.3 %copy-start.13 = (bf16[3,128,256]{2,1,0:T(8,128)(2,1)S(1)}, bf16[3,128,256]{2,1,0:T(8,128)(2,1)}, u32[]{:S(2)}) copy-start(bf16[3,128,256]{2,1,0:T(8,128)(2,1)} %param.10) | copy-start | bytes 589828
  11.8 35.4 %all-to-all-start.1 = ((bf16[128,128,2]{0,2,1:T(2,128)(2,1)}), bf16[128,128,2]{0,2,1:T(2,128)(2,1)S(1)}, u32[]{:S(2)}, u32[]{:S(2)}) async-start(bf16[128,128,2]{0,2,1:T(2,128)(2,1)} %bitcast.11), calls=%async_computation.1 | async-start | bytes 131072 | tf_op jit(solution)/shard_map/all_to_all | solution.py:182
  32.5 8.4 collective-permute-start
  36.9 1.0 copy-start.16
  38.6 0.8 copy-start.15
  39.6 2.1 copy-start.8
  47.2 28.5 %all-to-all-start = ((bf16[128,128,2]{0,2,1:T(2,128)(2,1)}), bf16[128,128,2]{0,2,1:T(2,128)(2,1)S(1)}, u32[]{:S(2)}, u32[]{:S(2)}) async-start(bf16[128,128,2]{0,2,1:T(2,128)(2,1)} %bitcast.1), calls=%async_computation | async-start | bytes 131072 | tf_op jit(solution)/shard_map/all_to_all | solution.py:181
  75.7 7.9 copy-start.2
  75.7 22.4 %all-to-all-start.3 = ((bf16[128,128,2]{0,2,1:T(2,128)(2,1)}), bf16[128,128,2]{0,2,1:T(2,128)(2,1)S(1)}, u32[]{:S(2)}, u32[]{:S(2)}) async-start(bf16[128,128,2]{0,2,1:T(2,128)(2,1)} %bitcast.28), calls=%async_computation.3 | async-start | bytes 131072 | tf_op jit(solution)/shard_map/all_to_all | solution.py:195
  103.6 1.0 copy-start.6
  103.7 1.0 copy-start.7
  110.4 22.3 %all-to-all-start.5 = ((bf16[128,128,2]{1,2,0:T(2,128)(2,1)}), bf16[128,128,2]{1,2,0:T(2,128)(2,1)}, u32[]{:S(2)}, u32[]{:S(2)}) async-start(bf16[128,128,2]{1,2,0:T(2,128)(2,1)} %bitcast.233), calls=%async_computation.5 | async-start | bytes 131072 | tf_op jit(solution)/shard_map/all_to_all | solution.py:203
  118.1 1.0 copy-start.1
  125.3 0.8 copy-start.3
  125.3 0.9 copy-start.5
  132.8 26.4 %all-to-all-start.4 = ((bf16[128,128,2]{1,2,0:T(2,128)(2,1)}), bf16[128,128,2]{1,2,0:T(2,128)(2,1)S(1)}, u32[]{:S(2)}, u32[]{:S(2)}) async-start(bf16[128,128,2]{1,2,0:T(2,128)(2,1)} %get-tuple-element.66), calls=%async_computation.4 | async-start | bytes 131072 | tf_op jit(solution)/shard_map/all_to_all | solution.py:202
  144.3 1037.2 %all-reduce.4.cloned.1.call-start = ((), (), s32[]{:S(2)}) async-start(), calls=%async_computation.6 | async-start | bytes 131072 | tf_op jit(solution)/shard_map/psum | solution.py:230
  159.2 21.9 %all-to-all-start.2 = ((bf16[128,128,2]{1,2,0:T(2,128)(2,1)}), bf16[128,128,2]{1,2,0:T(2,128)(2,1)S(1)}, u32[]{:S(2)}, u32[]{:S(2)}) async-start(bf16[128,128,2]{1,2,0:T(2,128)(2,1)} %get-tuple-element.67), calls=%async_computation.2 | async-start | bytes 131072 | tf_op jit(solution)/shard_map/all_to_all | solution.py:194
  166.3 14.8 %copy-start.9 = (bf16[128,256]{0,1:T(8,128)(2,1)S(1)}, bf16[128,256]{0,1:T(8,128)(2,1)}, u32[]{:S(2)}) copy-start(bf16[128,256]{0,1:T(8,128)(2,1)} %copy-done.8) | copy-start | bytes 196612
  181.2 3.4 copy-start.10
  181.2 103.2 %collective-permute-start.1 = (f32[3,2,256]{1,2,0:T(8,128)S(1)}, f32[3,2,256]{1,2,0:T(8,128)S(1)}, u32[]{:S(2)}, u32[]{:S(2)}) collective-permute-start(f32[3,2,256]{1,2,0:T(8,128)S(1)} %bitcast.248), channel_id=1, source_target_pairs={{4,0},{8,4},{12,8},{16,12},{20,16},{24,20},{28,24},{32,28},{36,32}... | collective-permute-start | bytes 18440 | tf_op jit(solution)/shard_map/ppermute | solution.py:14
  (7 other events, 4.9 us)
Sparse Core Ops, SparseCore 0:
  148.1 1033.4 all-reduce.3
where the time goes:
time: 1200 us; the launch traced here: 1190 us
  blocking collectives  703 us (59%)
  waiting for transfers between devices  352 us (29%)
  starting transfers between devices  74.6 us (6%)
  matrix products  26.9 us (2%)
  between operations  15.1 us (1%)
    psum x1, blocking collectives, on_device(): lax.psum((taps_part, grad_skip_part, last_part, rate_part), 'ctx')  604 us
    psum x1, waiting for transfers between devices, on_device(): lax.psum((taps_part, grad_skip_part, last_part, rate_part), 'ctx')  291 us
    psum x1, blocking collectives, on_device(): lax.psum((first_part, first_bias, second_part, second_bias), ('ctx', 'tp'))  99 us
  transfers between devices with their start and end apart: 9, of which 8 were waited for; matrix products, arithmetic and copies ran while one was open for 2% of the time, Pallas kernels for 0%

commit v1 on v0

v1 whole, which is shorter than its diff:
```python
import math

import jax
import jax.numpy as jnp
import ml_dtypes
import numpy as np
from jax import lax
from jax.experimental import pallas as pl
from jax.experimental.pallas import tpu as pltpu
from jax.sharding import PartitionSpec as P

F32 = jnp.float32
BF16 = jnp.bfloat16
BLK = 128
SIDE = 256
CHUNK = 2048
ONES_ROW = 33
LO_ROW = 36
HI_ROW = 69
VMEM = 56 * 1024 * 1024
NT = (((1,), (1,)), ((), ()))


def split_const(table):
    hi = table.astype(ml_dtypes.bfloat16)
    lo = (table - hi.astype(np.float64)).astype(ml_dtypes.bfloat16)
    return hi, lo


def dft_consts():
    total = SIDE * BLK
    k_row = np.arange(SIDE)[:, None]
    n_row = np.arange(BLK)[None, :]
    angle = 2 * np.pi * ((k_row * n_row) % SIDE) / SIDE
    rows = np.concatenate([np.cos(angle), -np.sin(angle)], axis=0)
    rows_hi, rows_lo = split_const(rows)
    fwd_rows = np.concatenate([rows_hi, rows_lo], axis=1)
    back_hi, back_lo = split_const(rows.T / total)
    idx = np.arange(BLK)
    angle = 2 * np.pi * ((idx[:, None] * idx[None, :]) % BLK) / BLK
    cos, sin = np.cos(angle), np.sin(angle)
    cols = np.concatenate(split_const(np.block([[cos, -sin], [sin, cos]])), axis=0)
    back_cols = np.concatenate(split_const(np.block([[cos, sin], [-sin, cos]])), axis=0)
    angle = 2 * np.pi * ((k_row * n_row) % total) / total
    twist = np.concatenate([np.cos(angle), np.sin(angle)], axis=1).astype(np.float32)
    back_rows = np.concatenate([back_hi, back_lo], axis=0)
    return fwd_rows, cols, twist, back_cols, back_rows


def feature_const(seq_len, bands):
    t = np.arange(seq_len)[None, :]
    k = np.arange(1, bands + 1)[:, None]
    angle = 2 * np.pi * ((k * t) % seq_len) / seq_len
    feat = np.concatenate([t / seq_len, np.cos(angle), np.sin(angle)], axis=0)
    hi, lo = split_const(feat)
    count = feat.shape[0]
    table = np.zeros((BLK, seq_len), ml_dtypes.bfloat16)
    table[:count] = hi
    table[ONES_ROW : ONES_ROW + 2] = 1
    table[LO_ROW : LO_ROW + count] = lo
    table[HI_ROW : HI_ROW + count] = hi
    return table


def fit_sin_cos():
    r = np.linspace(0.0, np.pi / 2 * 1.001, 4001)[1:]
    z = r * r
    s = np.linalg.lstsq(np.stack([z**i for i in range(6)], 1), np.sin(r) / r, rcond=None)[0]
    c = np.linalg.lstsq(np.stack([z**i for i in range(6)], 1), np.cos(r), rcond=None)[0]
    return [float(v) for v in s], [float(v) for v in c]


SIN_C, COS_C = fit_sin_cos()


def sin_cos(x):
    n = jnp.round(x * (1.0 / math.pi))
    r = (x - n * 3.140625) - n * 9.67653589793e-4
    parity = n - 2.0 * jnp.floor(n * 0.5)
    sign = 1.0 - 2.0 * parity
    z = r * r
    s = jnp.full_like(z, SIN_C[5])
    c = jnp.full_like(z, COS_C[5])
    for i in range(4, -1, -1):
        s = s * z + SIN_C[i]
        c = c * z + COS_C[i]
    return s * (r * sign), c * sign


def split(x):
    hi = x.astype(BF16)
    return hi, (x - hi.astype(F32)).astype(BF16)


def dot(a, b):
    return jnp.dot(a, b, preferred_element_type=F32)


def dot_nt(a, b, precision=None):
    return lax.dot_general(a, b, NT, preferred_element_type=F32, precision=precision)


def eye():
    row = lax.broadcasted_iota(jnp.int32, (BLK, BLK), 0)
    col = lax.broadcasted_iota(jnp.int32, (BLK, BLK), 1)
    return jnp.where(row == col, 1.0, 0.0).astype(BF16)


def forward_spectra(signals, fwd_rows, cols, twist):
    count = len(signals)
    xs = jnp.concatenate(signals, axis=1)
    inner = dot(fwd_rows[...], jnp.concatenate([xs, xs], axis=0))
    tc, ts = twist[:, :BLK], twist[:, BLK:]
    parts = []
    for s in range(count):
        re = inner[:SIDE, s * BLK : (s + 1) * BLK]
        im = inner[SIDE:, s * BLK : (s + 1) * BLK]
        parts.append(jnp.concatenate([re * tc + im * ts, im * tc - re * ts], axis=1))
    hi, lo = split(jnp.concatenate(parts, axis=0))
    c_hi, c_lo = cols[:SIDE, :], cols[SIDE:, :]
    spec = dot(hi, c_hi) + dot(lo, c_hi) + dot(hi, c_lo)
    return [spec[s * SIDE : (s + 1) * SIDE] for s in range(count)]


def inverse_spectra(spectra, back_cols, back_rows, twist):
    count = len(spectra)
    hi, lo = split(jnp.concatenate(spectra, axis=0))
    c_hi, c_lo = back_cols[:SIDE, :], back_cols[SIDE:, :]
    inner = dot(hi, c_hi) + dot(lo, c_hi) + dot(hi, c_lo)
    tc, ts = twist[:, :BLK], twist[:, BLK:]
    parts = []
    for s in range(count):
        re = inner[s * SIDE : (s + 1) * SIDE, :BLK]
        im = inner[s * SIDE : (s + 1) * SIDE, BLK:]
        parts.append(jnp.concatenate([re * tc - im * ts, im * tc + re * ts], axis=0))
    hi, lo = split(jnp.concatenate(parts, axis=1))
    r_hi, r_lo = back_rows[:BLK, :], back_rows[BLK:, :]
    out = dot(r_hi, hi) + dot(r_hi, lo) + dot(r_lo, hi)
    return [out[:, s * BLK : (s + 1) * BLK] for s in range(count)]


def times(a, b, conj_a):
    ar, ai = a[:, :BLK], a[:, BLK:]
    br, bi = b[:, :BLK], b[:, BLK:]
    if conj_a:
        return jnp.concatenate([ar * br + ai * bi, ar * bi - ai * br], axis=1)
    return jnp.concatenate([ar * br - ai * bi, ar * bi + ai * br], axis=1)


def places():
    row = lax.broadcasted_iota(jnp.int32, (BLK, BLK), 0)
    col = lax.broadcasted_iota(jnp.int32, (BLK, BLK), 1)
    return row, col


def earlier(x, m):
    row, col = places()
    r = pltpu.roll(x, m, 1)
    return jnp.where(col >= m, r, jnp.where(row >= 1, pltpu.roll(r, 1, 0), 0.0))


def later(x, m):
    row, col = places()
    r = pltpu.roll(x, BLK - m, 1)
    return jnp.where(
        col < BLK - m, r, jnp.where(row < BLK - 1, pltpu.roll(r, BLK - 1, 0), 0.0)
    )


def decay_window(own_ref, h):
    row, col = places()
    t = (row * BLK + col).astype(F32)
    rate = jnp.full((BLK, BLK), own_ref[10, h], F32)
    return jnp.sqrt(2.0 * rate) * jnp.exp(-rate * t), 0.5 / rate - t


def pack_kernel(streams_ref, cot_ref, out_ref):
    ident = eye()
    for i in range(4):
        block = cot_ref[...] if i == 3 else streams_ref[i]
        for h in range(2):
            turned = lax.dot_general(
                block[:, h * BLK : (h + 1) * BLK],
                ident,
                (((0,), (0,)), ((), ())),
                preferred_element_type=F32,
            )
            at = (i * 2 + h) * BLK
            out_ref[:, at : at + BLK] = turned.astype(BF16)


def net_kernel(feat_ref, w1_ref, w2_ref, b2_ref, wl_ref, a1_ref, c1_ref, a2_ref, c2_ref, raw_ref):
    one, cos_one = sin_cos(dot(w1_ref[...], feat_ref[...]))
    a1_ref[...] = one.astype(BF16)
    c1_ref[...] = cos_one.astype(BF16)
    hi, lo = split(one)
    pre_two = dot(w2_ref[...], jnp.concatenate([hi, lo, hi], axis=0)) + b2_ref[...]
    two, cos_two = sin_cos(pre_two)
    a2_ref[...] = two.astype(BF16)
    c2_ref[...] = cos_two.astype(BF16)
    for h in range(2):
        row = jnp.sum(wl_ref[:, h : h + 1] * two, axis=0, keepdims=True)
        for j in range(CHUNK // BLK):
            raw_ref[h, j : j + 1, :] = row[:, j * BLK : (j + 1) * BLK]


def filt_kernel(own_ref, raw_ref, fwd_rows, cols, twist, spec_ref):
    signals = [
        (raw_ref[h] * decay_window(own_ref, h)[0]).astype(BF16) for h in range(2)
    ]
    for h, spec in enumerate(forward_spectra(signals, fwd_rows, cols, twist)):
        spec_ref[h] = spec


def owner_kernel(
    own_ref,
    recv_ref,
    raw_ref,
    spec_ref,
    fwd_rows,
    cols,
    twist,
    back_cols,
    back_rows,
    feat_ref,
    w2_ref,
    wl_ref,
    a1_ref,
    c1_ref,
    a2_ref,
    c2_ref,
    back_ref,
    vec_ref,
    line_ref,
):
    xs, sides, cots, gated, grad_mixed = [], [], [], [], []
    for h in range(2):
        x = [
            recv_ref[:, (i * 2 + h) * BLK : (i * 2 + h + 1) * BLK].astype(F32) for i in range(4)
        ]
        shifted = [[x[i], earlier(x[i], 1), earlier(x[i], 2)] for i in range(3)]
        side = [
            own_ref[i * 3, h] * shifted[i][0]
            + own_ref[i * 3 + 1, h] * shifted[i][1]
            + own_ref[i * 3 + 2, h] * shifted[i][2]
            for i in range(3)
        ]
        xs.append(shifted)
        sides.append(side)
        cots.append(x[3])
        gated.append((side[1] * side[2]).astype(BF16))
        grad_mixed.append((x[3] * side[0]).astype(BF16))
    spec = forward_spectra(gated + grad_mixed, fwd_rows, cols, twist)
    products = (
        [times(spec[h], spec[2 + h], True) for h in range(2)]
        + [times(spec[h], spec_ref[h], False) for h in range(2)]
        + [times(spec_ref[h], spec[2 + h], True) for h in range(2)]
    )
    convs = inverse_spectra(products, back_cols, back_rows, twist)

    sums = []
    line_ref[...] = jnp.zeros_like(line_ref)
    for h in range(2):
        grad_filt = convs[h].astype(BF16).astype(F32)
        window, slope = decay_window(own_ref, h)
        grad_raw = grad_filt * window
        sums.append(jnp.sum(grad_raw * raw_ref[h] * slope, axis=0, keepdims=True))
        for n in range(BLK):
            line_ref[h : h + 1, n * BLK : (n + 1) * BLK] = grad_raw[n : n + 1, :]

    w2_hi, w2_lo = split(w2_ref[...])
    w2_stack = jnp.concatenate([w2_hi, w2_hi, w2_lo], axis=1)
    col0 = wl_ref[:, 0:1]
    col1 = wl_ref[:, 1:2]
    shared = jnp.zeros((112, BLK), F32)
    last = jnp.zeros((16, 64), F32)
    for j in range(line_ref.shape[1] // CHUNK):
        at = slice(j * CHUNK, (j + 1) * CHUNK)
        line = line_ref[:, at]
        grad_two = (col0 * line[0:1] + col1 * line[1:2]) * c2_ref[:, at].astype(F32)
        hi, lo = split(grad_two)
        grad_one = dot(w2_stack, jnp.concatenate([hi, lo, hi], axis=0)) * c1_ref[
            :, at
        ].astype(F32)
        left = jnp.concatenate([a1_ref[:, at], feat_ref[0:48, at]], axis=0)
        right = jnp.concatenate([hi, grad_one.astype(BF16)], axis=0)
        shared = shared + dot_nt(left, right)
        line_hi, line_lo = split(line)
        last = last + dot_nt(jnp.concatenate([line_hi, line_lo], axis=0), a2_ref[:, at])

    last = last[:8] + last[8:]
    count = 33
    biases = shared[64 + ONES_ROW : 64 + ONES_ROW + 1]
    low = jnp.concatenate(
        [
            shared[64 : 64 + count, 64:],
            biases[:, 64:],
            biases[:, :64],
            jnp.zeros((64 - count - 2, 64), F32),
        ],
        axis=0,
    )
    packed = jnp.concatenate([shared[:64, :64], low], axis=1).T
    p_hi, p_lo = split(packed)
    back_ref[:, 8 * BLK : 9 * BLK] = jnp.concatenate([p_hi, p_lo], axis=1)
    back_ref[:, 9 * BLK :] = jnp.zeros((BLK, BLK), BF16)

    for h in range(2):
        gain = own_ref[9, h]
        g = gated[h].astype(F32)
        gm = grad_mixed[h].astype(F32)
        mixed = (convs[2 + h] + gain * g).astype(BF16).astype(F32)
        grad_gated = (convs[4 + h] + gain * gm).astype(BF16).astype(F32)
        side = sides[h]
        grad_side = [cots[h] * mixed, grad_gated * side[2], grad_gated * side[1]]
        back_ref[:, h * BLK : (h + 1) * BLK] = (side[0] * mixed).astype(BF16)
        sums.append(jnp.sum(gm * g, axis=0, keepdims=True))
        for i in range(3):
            grad_stream = own_ref[i * 3, h] * grad_side[i]
            for m in range(1, 3):
                grad_stream = grad_stream + own_ref[i * 3 + m, h] * later(grad_side[i], m)
            at = (2 + i * 2 + h) * BLK
            back_ref[:, at : at + BLK] = grad_stream.astype(BF16)
            for m in range(3):
                sums.append(jnp.sum(grad_side[i] * xs[h][i][m], axis=0, keepdims=True))
    sums = jnp.concatenate(sums + [jnp.zeros((64 - len(sums), BLK), F32)], axis=0)
    totals = dot_nt(jnp.ones((8, BLK), F32), sums, lax.Precision.HIGHEST)
    vec_ref[...] = jnp.concatenate(
        [jnp.zeros((1, 64), F32), last[0:1], last[1:2], totals[0:1]], axis=1
    )


def unpack_kernel(recv_ref, out_ref, grad_ref):
    ident = eye()
    for i in range(4):
        for h in range(2):
            at = (i * 2 + h) * BLK
            turned = lax.dot_general(
                recv_ref[:, at : at + BLK],
                ident,
                (((0,), (0,)), ((), ())),
                preferred_element_type=F32,
            ).astype(BF16)
            if i == 0:
                out_ref[:, h * BLK : (h + 1) * BLK] = turned
            else:
                grad_ref[i - 1, :, h * BLK : (h + 1) * BLK] = turned


def final_kernel(
    all_ref, taps_ref, w1_ref, b1_ref, w2_ref, b2_ref, wl_ref, rate_ref, skip_ref
):
    low = all_ref[:, :BLK].T
    high = all_ref[:, BLK:].T
    shared = low[:64]
    flipped = shared[:, 64:]
    w2_ref[...] = shared[:, :64]
    w1_ref[...] = flipped[:33]
    b1_ref[...] = flipped[33:34]
    b2_ref[...] = flipped[34:35]
    wl_ref[:, :BLK] = low[64:]
    wl_ref[:, BLK:] = high[:64]
    rest = high[64:]
    for h in range(2):
        at = slice(h * BLK, (h + 1) * BLK)
        rate_ref[:, at] = rest[h : h + 1]
        skip_ref[:, at] = rest[2 + 10 * h : 3 + 10 * h]
        taps_ref[:, at] = rest[3 + 10 * h : 12 + 10 * h]


def params(**kwargs):
    return pltpu.CompilerParams(vmem_limit_bytes=VMEM, **kwargs)


def stacked_weights(weights, order):
    hi = lax.reduce_precision(weights, 8, 7)
    lo = weights - hi
    return jnp.concatenate([lo if name == "lo" else hi for name in order], axis=0)


def on_device(
    streams,
    short_taps,
    w_first,
    b_first,
    w_second,
    b_second,
    w_last,
    decay_rate,
    skip_gain,
    cotangent,
):
    peers = lax.axis_size("ctx")
    rank = lax.axis_index("ctx")
    tok = streams.shape[1]
    channels = streams.shape[2]
    seq_len = tok * peers
    count, hid = w_first.shape
    vmem = pl.BlockSpec(memory_space=pltpu.VMEM)
    smem = pl.BlockSpec(memory_space=pltpu.SMEM)
    shape = jax.ShapeDtypeStruct

    outgoing = pl.pallas_call(
        pack_kernel,
        out_shape=shape((peers, 8 * tok), BF16),
        name="pack_rows",
    )(streams, cotangent)
    incoming = lax.all_to_all(
        outgoing.reshape(peers, 8, tok), "ctx", split_axis=0, concat_axis=0, tiled=True
    ).reshape(peers, 8 * tok)

    table = jnp.concatenate(
        [short_taps.reshape(9, channels), skip_gain[None], decay_rate[None], w_last], axis=0
    )
    own = lax.dynamic_index_in_dim(
        table.reshape(11 + hid, 2, peers), rank, axis=2, keepdims=False
    )
    own_wl = own[11:]
    fwd_rows, cols, twist, back_cols, back_rows = (jnp.asarray(c) for c in dft_consts())
    feat = jnp.asarray(feature_const(seq_len, (count - 1) // 2))
    b_hi = lax.reduce_precision(b_first, 8, 7)
    w_hi = lax.reduce_precision(w_first, 8, 7)
    w1 = (
        jnp.concatenate(
            [
                w_hi,
                b_hi[None],
                (b_first - b_hi)[None],
                jnp.zeros((LO_ROW - ONES_ROW - 2, hid), F32),
                w_hi,
                w_first - w_hi,
                jnp.zeros((BLK - HI_ROW - count, hid), F32),
            ],
            axis=0,
        )
        .T.astype(BF16)
    )
    w2_hi = lax.reduce_precision(w_second, 8, 7)
    w2 = jnp.concatenate([w2_hi, w2_hi, w_second - w2_hi], axis=0).T.astype(BF16)

    act = shape((hid, seq_len), BF16)
    act_spec = pl.BlockSpec((hid, CHUNK), lambda j: (0, j))
    whole = lambda *dims: pl.BlockSpec(dims, lambda j: (0,) * len(dims))
    a1, c1, a2, c2, raw = pl.pallas_call(
        net_kernel,
        grid=(seq_len // CHUNK,),
        in_specs=[
            pl.BlockSpec((BLK, CHUNK), lambda j: (0, j)),
            whole(hid, BLK),
            whole(hid, 3 * hid),
            whole(hid, 1),
            whole(hid, 2),
        ],
        out_specs=[
            act_spec,
            act_spec,
            act_spec,
            act_spec,
            pl.BlockSpec((2, CHUNK // BLK, BLK), lambda j: (0, j, 0)),
        ],
        out_shape=[act, act, act, act, shape((2, BLK, BLK), F32)],
        compiler_params=params(dimension_semantics=("arbitrary",)),
        name="filter_net",
    )(feat, w1, w2, b_second[:, None], own_wl)
    filt_spec = pl.pallas_call(
        filt_kernel,
        in_specs=[smem] + [vmem] * 4,
        out_specs=vmem,
        out_shape=shape((2, SIDE, SIDE), F32),
        compiler_params=params(),
        name="filter_spectrum",
    )(own, raw, fwd_rows, cols, twist)

    back, vec = pl.pallas_call(
        owner_kernel,
        in_specs=[smem] + [vmem] * 15,
        out_specs=[vmem, vmem],
        out_shape=[shape((peers, 10 * tok), BF16), shape((1, 2 * BLK), F32)],
        scratch_shapes=[pltpu.VMEM((8, seq_len), F32)],
        compiler_params=params(),
        name="convolve_channels",
    )(
        own,
        incoming,
        raw,
        filt_spec,
        fwd_rows,
        cols,
        twist,
        back_cols,
        back_rows,
        feat,
        w_second,
        own_wl,
        a1,
        c1,
        a2,
        c2,
    )
    returned = lax.all_to_all(
        back.reshape(peers, 2, 5 * tok), "ctx", split_axis=0, concat_axis=0, tiled=True
    ).reshape(peers, 10 * tok)
    halves = jnp.sum(returned[:, 8 * tok : 9 * tok].astype(F32), axis=0)
    mine = lax.psum(halves[:64] + halves[64:], "tp")
    vec = jnp.concatenate([mine[None], vec[:, 64:]], axis=1)
    spread = jnp.broadcast_to(vec, (peers, 2 * BLK))
    gathered = lax.all_to_all(spread, "ctx", split_axis=0, concat_axis=0, tiled=True)
    output, grad_streams = pl.pallas_call(
        unpack_kernel,
        out_shape=[shape((tok, channels), BF16), shape((3, tok, channels), BF16)],
        name="unpack_rows",
    )(returned)
    taps, gw1, gb1, gw2, gb2, gwl, rate, skip = pl.pallas_call(
        final_kernel,
        out_shape=[
            shape((9, channels), F32),
            shape((count, hid), F32),
            shape((1, hid), F32),
            shape((hid, hid), F32),
            shape((1, hid), F32),
            shape((hid, channels), F32),
            shape((1, channels), F32),
            shape((1, channels), F32),
        ],
        name="unpack_sums",
    )(gathered)
    return (
        output,
        grad_streams,
        taps.reshape(3, 3, channels),
        gw1,
        gb1[0],
        gw2,
        gb2[0],
        gwl,
        rate[0],
        skip[0],
    )


def solution(mesh):
    return jax.shard_map(
        on_device,
        mesh=mesh,
        in_specs=(
            P(None, "ctx", "tp"),
            P(None, None, "tp"),
            P(),
            P(),
            P(),
            P(),
            P(None, "tp"),
            P("tp"),
            P("tp"),
            P("ctx", "tp"),
        ),
        out_specs=(
            P("ctx", "tp"),
            P(None, "ctx", "tp"),
            P(None, None, "tp"),
            P(),
            P(),
            P(),
            P(),
            P(None, "tp"),
            P("tp"),
            P("tp"),
        ),
        check_vma=False,
    )
```

time: 1200 us -> 147 us (0.12)
  the two profiles are of different devices: /device:TPU:2 before, /device:TPU:4 now
where the time goes in v1:
time: 147 us
  starting transfers between devices  43.8 us (30%)
  waiting for transfers between devices  40.8 us (28%)
  Pallas kernels  36.2 us (25%)
  local copies, waits for them, and re-layouts  15.5 us (11%)
  blocking collectives  7.14 us (5%)
  other arithmetic  2.38 us (2%)
    all_to_all x1, waiting for transfers between devices, on_device(): lax.all_to_all(back.reshape(peers, 2, 5 * tok), 'ctx', split_axis=0, conc...  24.5 us
    all_to_all x1, starting transfers between devices, on_device(): lax.all_to_all(outgoing.reshape(peers, 8, tok), 'ctx', split_axis=0, conc...  20.6 us
    all_to_all x1, starting transfers between devices, on_device(): lax.all_to_all(back.reshape(peers, 2, 5 * tok), 'ctx', split_axis=0, conc...  17.1 us
    all_to_all x1, waiting for transfers between devices, on_device(): lax.all_to_all(spread, 'ctx', split_axis=0, concat_axis=0, tiled=True)  16.3 us
    pallas_call x1, Pallas kernels, on_device(): pl.pallas_call(net_kernel, grid=(seq_len // CHUNK,), in_specs=[pl.BlockSp...  15 us
    pallas_call x1, Pallas kernels, on_device(): pl.pallas_call(owner_kernel, in_specs=[smem] + [vmem] * 15, out_specs=[vm...  12.7 us
    psum x1, blocking collectives, on_device(): mine = lax.psum(halves[:64] + halves[64:], 'tp')  7.14 us
    all_to_all x1, starting transfers between devices, on_device(): lax.all_to_all(spread, 'ctx', split_axis=0, concat_axis=0, tiled=True)  6.19 us
  transfers between devices with their start and end apart: 3, of which 2 were waited for; matrix products, arithmetic and copies ran while one was open for 7% of the time, Pallas kernels for 14%

profile of v1, /device:TPU:4, one launch (start us, length us, event | category | flops | bytes accessed | tf_op | source)
XLA Modules:
  0.0 146.6 jit_solution(9121142243943834685)
XLA Ops:
  0.7 1.9 %pack_rows.1 = bf16[128,1024]{1,0:T(8,128)(2,1)} custom-call(bf16[3,128,256]{2,1,0:T(8,128)(2,1)} %streams_ref.1, bf16[128,256]{1,0:T(8,128)(2,1)} %cot_ref.1), custom_call_target="tpu_custom_call" | custom-call | tf_op jit(solution)/shard_map/pack_rows/pallas_call | solution.py:403
  2.6 1.7 %copy.82 = bf16[16,8,8,128]{3,2,1,0:T(8,128)(2,1)} copy(bf16[16,8,8,128]{3,1,2,0:T(8,128)(2,1)} %bitcast.36) | data formatting | bytes 524288
  4.3 20.6 %all-to-all-start = ((bf16[128,8,128]{2,1,0:T(8,128)(2,1)}), bf16[128,8,128]{2,1,0:T(8,128)(2,1)S(1)}, u32[]{:S(2)}, u32[]{:S(2)}) async-start(bf16[128,8,128]{2,1,0:T(8,128)(2,1)} %bitcast.17), calls=%async_computation | async-start | bytes 524288 | tf_op jit(solution)/shard_map/all_to_all | solution.py:408
  24.9 0.7 reduce_precision.9
  25.6 0.8 copy.72
  26.4 0.7 concatenate.25
  28.1 1.4 copy.78.b2_ref
  29.5 0.8 copy.76
  30.3 0.9 concatenate.28
  31.9 0.7 copy.70
  34.9 15.0 %filter_net.1 = (bf16[64,16384]{1,0:T(8,128)(2,1)}, bf16[64,16384]{1,0:T(8,128)(2,1)}, bf16[64,16384]{1,0:T(8,128)(2,1)}, bf16[64,16384]{1,0:T(8,128)(2,1)}, f32[2,128,128]{2,1,0:T(8,128)}) custom-call(bf16[128,16384]{1,0:T(8,128)(2,1)} %constant.35.clone.feat_ref, bf16[64,128]{1,0:T(8,128)(2,1)} %bitcast.40, bf16[64,192]{1,0:T(8,128)(2,1)} %maximum_bitcast_fusion.w2_ref, ...), custom_call_target="tpu_custom_call" | custom-call | tf_op jit(solution)/shard_map/filter_net/pallas_call | solution.py:444
  49.8 3.0 %filter_spectrum.1.spec_ref = f32[2,256,256]{2,1,0:T(8,128)} custom-call(f32[75,2]{1,0:T(8,128)} %bitcast.38, f32[2,128,128]{2,1,0:T(8,128)} %get-tuple-element.27.raw_ref, bf16[512,256]{1,0:T(8,128)(2,1)} %constant.30.clone.fwd_rows, bf16[512,256]{1,0:T(8,128)(2,1)} %constant.31.clone.cols, f32[256,256]{1,0:T(8,128)} %constant.32.clone.twist), custom_call_target="tpu_custom_call" | custom-call | tf_op jit(solution)/shard_map/filter_spectrum/pallas_call | solution.py:465
  52.8 0.8 copy.87
  53.6 12.7 %convolve_channels.1 = (bf16[128,1280]{1,0:T(8,128)(2,1)}, f32[1,256]{1,0:T(1,128)}) custom-call(f32[75,2]{1,0:T(8,128)} %bitcast.39, bf16[128,1024]{1,0:T(8,128)(2,1)} %bitcast.34, f32[2,128,128]{2,1,0:T(8,128)} %get-tuple-element.27.raw_ref, f32[2,256,256]{2,1,0:T(8,128)} %filter_spectrum.1.spec_ref, bf16[512,256]{1,0:T(8,128)(2,1)} %constant.30.clone.fwd_rows, ...), custom_call_target="tpu_custom_call" | custom-call | tf_op jit(solution)/shard_map/convolve_channels/pallas_call | solution.py:474
  66.3 1.8 %reshape.53 = bf16[128,2,640]{2,1,0:T(2,128)(2,1)} reshape(bf16[128,1280]{1,0:T(8,128)(2,1)} %get-tuple-element.32) | data formatting | bytes 655360 | tf_op jit(solution)/shard_map/reshape | solution.py:501
  68.1 17.1 %all-to-all-start.1 = ((bf16[128,2,640]{2,1,0:T(2,128)(2,1)}), bf16[128,2,640]{2,1,0:T(2,128)(2,1)S(1)}, u32[]{:S(2)}, u32[]{:S(2)}) async-start(bf16[128,2,640]{2,1,0:T(2,128)(2,1)} %reshape.53), calls=%async_computation.1 | async-start | bytes 655360 | tf_op jit(solution)/shard_map/all_to_all | solution.py:500
  85.1 0.8 slice.23
  85.9 24.5 %all-to-all-done.1 = bf16[128,2,640]{2,1,0:T(2,128)(2,1)S(1)} async-done(((bf16[128,2,640]{2,1,0:T(2,128)(2,1)}), bf16[128,2,640]{2,1,0:T(2,128)(2,1)S(1)}, u32[]{:S(2)}, u32[]{:S(2)}) %all-to-all-start.1) | async-done | bytes 327712 | tf_op jit(solution)/shard_map/all_to_all | solution.py:500
  110.5 7.1 %psum.7 = f32[1,64]{1,0:T(1,128)S(1)} all-reduce(f32[1,64]{1,0:T(1,128)S(1)} %add_bitcast_fusion), channel_id=1, replica_groups=mesh['ctx'=128,'tp'=4] {'tp'}, use_global_device_ids=true, to_apply=%region_1.2 | all-reduce | flops 64 | bytes 512 | tf_op jit(solution)/shard_map/psum | solution.py:504
  118.5 6.2 %all-to-all-start.2 = ((f32[128,1,256]{2,1,0:T(1,128)}), f32[128,1,256]{2,1,0:T(1,128)S(1)}, u32[]{:S(2)}, u32[]{:S(2)}) async-start(f32[128,1,256]{2,1,0:T(1,128)} %broadcast_in_dim.33), calls=%async_computation.2 | async-start | bytes 262144 | tf_op jit(solution)/shard_map/all_to_all | solution.py:507
  124.7 1.9 %unpack_rows.1 = (bf16[128,256]{1,0:T(8,128)(2,1)}, bf16[3,128,256]{2,1,0:T(8,128)(2,1)}) custom-call(bf16[128,1280]{1,0:T(8,128)(2,1)} %bitcast.32), custom_call_target="tpu_custom_call" | custom-call | tf_op jit(solution)/shard_map/unpack_rows/pallas_call | solution.py:508
  126.6 16.3 %all-to-all-done.2 = f32[128,1,256]{2,1,0:T(1,128)S(1)} async-done(((f32[128,1,256]{2,1,0:T(1,128)}), f32[128,1,256]{2,1,0:T(1,128)S(1)}, u32[]{:S(2)}, u32[]{:S(2)}) %all-to-all-start.2) | async-done | bytes 131104 | tf_op jit(solution)/shard_map/all_to_all | solution.py:507
  143.6 1.7 %unpack_sums.1 = (f32[9,256]{1,0:T(8,128)}, f32[33,64]{1,0:T(8,128)}, f32[1,64]{1,0:T(1,128)}, f32[64,64]{1,0:T(8,128)}, f32[1,64]{1,0:T(1,128)}, /*index=5*/f32...) custom-call(f32[128,256]{1,0:T(8,128)} %bitcast.37), custom_call_target="tpu_custom_call" | custom-call | tf_op jit(solution)/shard_map/unpack_sums/pallas_call | solution.py:513
  145.3 1.3 reshape.55
  (30 shorter events, 5.5 us)
Async XLA Ops:
  0.6 30.8 %copy-start.1 = (f32[256]{0:T(256)S(1)}, f32[256]{0:T(256)}, u32[]{:S(2)}) copy-start(f32[256]{0:T(256)} %param.23) | copy-start | bytes 3076
  0.7 31.0 %copy-start.2 = (f32[256]{0:T(256)S(1)}, f32[256]{0:T(256)}, u32[]{:S(2)}) copy-start(f32[256]{0:T(256)} %param.24) | copy-start | bytes 3076
  4.3 48.5 %all-to-all-start = ((bf16[128,8,128]{2,1,0:T(8,128)(2,1)}), bf16[128,8,128]{2,1,0:T(8,128)(2,1)S(1)}, u32[]{:S(2)}, u32[]{:S(2)}) async-start(bf16[128,8,128]{2,1,0:T(8,128)(2,1)} %bitcast.17), calls=%async_computation | async-start | bytes 524288 | tf_op jit(solution)/shard_map/all_to_all | solution.py:408
  68.1 42.3 %all-to-all-start.1 = ((bf16[128,2,640]{2,1,0:T(2,128)(2,1)}), bf16[128,2,640]{2,1,0:T(2,128)(2,1)S(1)}, u32[]{:S(2)}, u32[]{:S(2)}) async-start(bf16[128,2,640]{2,1,0:T(2,128)(2,1)} %reshape.53), calls=%async_computation.1 | async-start | bytes 655360 | tf_op jit(solution)/shard_map/all_to_all | solution.py:500
  110.4 14.3 %copy-start = (bf16[16,8,2,640]{3,1,2,0:T(8,128)(2,1)}, bf16[16,8,2,640]{3,1,2,0:T(8,128)(2,1)S(1)}, u32[]{:S(2)}) copy-start(bf16[16,8,2,640]{3,1,2,0:T(8,128)(2,1)S(1)} %copy.84) | copy-start | bytes 983044
  118.5 24.4 %all-to-all-start.2 = ((f32[128,1,256]{2,1,0:T(1,128)}), f32[128,1,256]{2,1,0:T(1,128)S(1)}, u32[]{:S(2)}, u32[]{:S(2)}) async-start(f32[128,1,256]{2,1,0:T(1,128)} %broadcast_in_dim.33), calls=%async_computation.2 | async-start | bytes 262144 | tf_op jit(solution)/shard_map/all_to_all | solution.py:507

commit v2 on v1

--- a/solution.py
+++ b/solution.py
@@ -63,28 +63,25 @@
 
 
 def fit_sin_cos():
-    r = np.linspace(0.0, np.pi / 2 * 1.001, 4001)[1:]
+    r = np.cos(np.linspace(0.0, np.pi / 2, 4001))[:-1]
+    powers = np.stack([r ** (2 * i) for i in range(6)], 1)
+    s = np.linalg.lstsq(powers * r[:, None], np.sin(np.pi * r), rcond=None)[0]
+    c = np.linalg.lstsq(powers, np.cos(np.pi * r), rcond=None)[0]
+    return [float(v) for v in s], [float(v) for v in c]
+
+
+SIN_C, COS_C = fit_sin_cos()
+
+
+def sin_cos_pi(x):
+    r = x - 2.0 * jnp.round(x * 0.5)
     z = r * r
-    s = np.linalg.lstsq(np.stack([z**i for i in range(6)], 1), np.sin(r) / r, rcond=None)[0]
-    c = np.linalg.lstsq(np.stack([z**i for i in range(6)], 1), np.cos(r), rcond=None)[0]
-    return [float(v) for v in s], [float(v) for v in c]
-
-
-SIN_C, COS_C = fit_sin_cos()
-
-
-def sin_cos(x):
-    n = jnp.round(x * (1.0 / math.pi))
-    r = (x - n * 3.140625) - n * 9.67653589793e-4
-    parity = n - 2.0 * jnp.floor(n * 0.5)
-    sign = 1.0 - 2.0 * parity
-    z = r * r
-    s = jnp.full_like(z, SIN_C[5])
-    c = jnp.full_like(z, COS_C[5])
-    for i in range(4, -1, -1):
+    s = SIN_C[5] * z + SIN_C[4]
+    c = COS_C[5] * z + COS_C[4]
+    for i in range(3, -1, -1):
         s = s * z + SIN_C[i]
         c = c * z + COS_C[i]
-    return s * (r * sign), c * sign
+    return s * r, c
 
 
 def split(x):
@@ -122,9 +119,14 @@
     return [spec[s * SIDE : (s + 1) * SIDE] for s in range(count)]
 
 
-def inverse_spectra(spectra, back_cols, back_rows, twist):
-    count = len(spectra)
-    hi, lo = split(jnp.concatenate(spectra, axis=0))
+def inverse_pairs(pairs, back_cols, back_rows, twist):
+    joined = []
+    for a, b in pairs:
+        joined.append(
+            jnp.concatenate([a[:, :BLK] - b[:, BLK:], a[:, BLK:] + b[:, :BLK]], axis=1)
+        )
+    count = len(pairs)
+    hi, lo = split(jnp.concatenate(joined, axis=0))
     c_hi, c_lo = back_cols[:SIDE, :], back_cols[SIDE:, :]
     inner = dot(hi, c_hi) + dot(lo, c_hi) + dot(hi, c_lo)
     tc, ts = twist[:, :BLK], twist[:, BLK:]
@@ -132,11 +134,14 @@
     for s in range(count):
         re = inner[s * SIDE : (s + 1) * SIDE, :BLK]
         im = inner[s * SIDE : (s + 1) * SIDE, BLK:]
-        parts.append(jnp.concatenate([re * tc - im * ts, im * tc + re * ts], axis=0))
+        tr = re * tc - im * ts
+        ti = im * tc + re * ts
+        parts.append(jnp.concatenate([tr, ti], axis=0))
+        parts.append(jnp.concatenate([ti, -tr], axis=0))
     hi, lo = split(jnp.concatenate(parts, axis=1))
     r_hi, r_lo = back_rows[:BLK, :], back_rows[BLK:, :]
     out = dot(r_hi, hi) + dot(r_hi, lo) + dot(r_lo, hi)
-    return [out[:, s * BLK : (s + 1) * BLK] for s in range(count)]
+    return [out[:, s * BLK : (s + 1) * BLK] for s in range(2 * count)]
 
 
 def times(a, b, conj_a):
@@ -167,53 +172,109 @@
     )
 
 
-def decay_window(own_ref, h):
+def picked(x, rank):
+    lane = lax.broadcasted_iota(jnp.int32, x.shape, 1)
+    return jnp.sum(jnp.where(lane == rank, x, 0.0), axis=1, keepdims=True)
+
+
+def half(h):
+    return slice(h * BLK, (h + 1) * BLK)
+
+
+def decay_window(rate_ref, rank, h):
     row, col = places()
     t = (row * BLK + col).astype(F32)
-    rate = jnp.full((BLK, BLK), own_ref[10, h], F32)
+    rate = jnp.broadcast_to(picked(rate_ref[:, half(h)], rank), (BLK, BLK))
     return jnp.sqrt(2.0 * rate) * jnp.exp(-rate * t), 0.5 / rate - t
 
 
-def pack_kernel(streams_ref, cot_ref, out_ref):
-    ident = eye()
+def turned(block):
+    return lax.dot_general(
+        block, eye(), (((0,), (0,)), ((), ())), preferred_element_type=F32
+    )
+
+
+def pack_kernel(streams_ref, cot_ref, out_ref, hold_ref):
     for i in range(4):
         block = cot_ref[...] if i == 3 else streams_ref[i]
         for h in range(2):
-            turned = lax.dot_general(
-                block[:, h * BLK : (h + 1) * BLK],
-                ident,
-                (((0,), (0,)), ((), ())),
-                preferred_element_type=F32,
+            hold_ref[:, i * 2 + h, :] = turned(block[:, half(h)])
+    out_ref[...] = hold_ref[...].astype(BF16)
+
+
+def net_kernel(
+    rank_ref,
+    feat_ref,
+    w1_ref,
+    b1_ref,
+    w2_ref,
+    b2_ref,
+    wl_ref,
+    a1_ref,
+    c1_ref,
+    a2_ref,
+    c2_ref,
+    raw_ref,
+    w1_hold,
+    w2_hold,
+    wl_hold,
+):
+    @pl.when(pl.program_id(0) == 0)
+    def _():
+        def parts(ref):
+            x = ref[...] * (1.0 / math.pi)
+            hi = x.astype(BF16).astype(F32)
+            return hi, x - hi
+
+        w_hi, w_lo = parts(w1_ref)
+        b_hi, b_lo = parts(b1_ref)
+        count, hid = w_hi.shape
+        gap = jnp.zeros((LO_ROW - ONES_ROW - 2, hid), F32)
+        end = jnp.zeros((BLK - HI_ROW - count, hid), F32)
+        stack = jnp.concatenate([w_hi, b_hi, b_lo, gap, w_hi, w_lo, end], axis=0)
+        w1_hold[...] = stack.T.astype(BF16)
+        w_hi, w_lo = parts(w2_ref)
+        b_hi, b_lo = parts(b2_ref)
+        end = jnp.zeros((14, hid), F32)
+        stack = jnp.concatenate([w_hi, w_hi, w_lo, b_hi, b_lo, end], axis=0)
+        w2_hold[...] = stack.T.astype(BF16)
+        rank = rank_ref[0]
+        for h in range(2):
+            wl_hold[:, half(h)] = jnp.broadcast_to(
+                picked(wl_ref[:, half(h)], rank), (hid, BLK)
             )
-            at = (i * 2 + h) * BLK
-            out_ref[:, at : at + BLK] = turned.astype(BF16)
-
-
-def net_kernel(feat_ref, w1_ref, w2_ref, b2_ref, wl_ref, a1_ref, c1_ref, a2_ref, c2_ref, raw_ref):
-    one, cos_one = sin_cos(dot(w1_ref[...], feat_ref[...]))
+
+    one, cos_one = sin_cos_pi(dot(w1_hold[...], feat_ref[...]))
     a1_ref[...] = one.astype(BF16)
     c1_ref[...] = cos_one.astype(BF16)
     hi, lo = split(one)
-    pre_two = dot(w2_ref[...], jnp.concatenate([hi, lo, hi], axis=0)) + b2_ref[...]
-    two, cos_two = sin_cos(pre_two)
+    ones = jnp.ones((16, CHUNK), BF16)
+    two, cos_two = sin_cos_pi(dot(w2_hold[...], jnp.concatenate([hi, lo, hi, ones], axis=0)))
     a2_ref[...] = two.astype(BF16)
     c2_ref[...] = cos_two.astype(BF16)
     for h in range(2):
-        row = jnp.sum(wl_ref[:, h : h + 1] * two, axis=0, keepdims=True)
+        col = wl_hold[:, h * BLK : h * BLK + 1]
+        row = jnp.sum(col * two, axis=0, keepdims=True)
         for j in range(CHUNK // BLK):
             raw_ref[h, j : j + 1, :] = row[:, j * BLK : (j + 1) * BLK]
 
 
-def filt_kernel(own_ref, raw_ref, fwd_rows, cols, twist, spec_ref):
+def filt_kernel(rank_ref, rate_ref, raw_ref, fwd_rows, cols, twist, spec_ref):
     signals = [
-        (raw_ref[h] * decay_window(own_ref, h)[0]).astype(BF16) for h in range(2)
+        (raw_ref[h] * decay_window(rate_ref, rank_ref[0], h)[0]).astype(BF16)
+        for h in range(2)
     ]
     for h, spec in enumerate(forward_spectra(signals, fwd_rows, cols, twist)):
         spec_ref[h] = spec
 
 
 def owner_kernel(
-    own_ref,
+    rank_ref,
+    taps_ref,
+    skip_ref,
+    rate_ref,
+    w2_ref,
+    wl_ref,
     recv_ref,
     raw_ref,
     spec_ref,
@@ -222,27 +283,52 @@
     twist,
     back_cols,
     back_rows,
+    feat_any,
+    a1_any,
+    c1_any,
+    a2_any,
+    c2_any,
+    back_ref,
+    vec_ref,
+    line_ref,
+    hold_ref,
     feat_ref,
-    w2_ref,
-    wl_ref,
     a1_ref,
     c1_ref,
     a2_ref,
     c2_ref,
-    back_ref,
-    vec_ref,
-    line_ref,
+    sems,
 ):
+    moves = [
+        pltpu.make_async_copy(src, dst, sems.at[k])
+        for k, (src, dst) in enumerate(
+            [
+                (c2_any, c2_ref),
+                (c1_any, c1_ref),
+                (a1_any, a1_ref),
+                (feat_any.at[pl.ds(0, 48), :], feat_ref),
+                (a2_any, a2_ref),
+            ]
+        )
+    ]
+    for move in moves:
+        move.start()
+    rank = rank_ref[0]
+    hold_ref[...] = recv_ref[...].astype(F32)
+    taps, gains = [], []
     xs, sides, cots, gated, grad_mixed = [], [], [], [], []
     for h in range(2):
-        x = [
-            recv_ref[:, (i * 2 + h) * BLK : (i * 2 + h + 1) * BLK].astype(F32) for i in range(4)
-        ]
+        gains.append(picked(skip_ref[:, half(h)], rank))
+        taps.append([])
+        for i in range(3):
+            own = picked(taps_ref[i, :, half(h)], rank)
+            taps[h].append([own[m : m + 1] for m in range(3)])
+        x = [hold_ref[:, i * 2 + h, :] for i in range(4)]
         shifted = [[x[i], earlier(x[i], 1), earlier(x[i], 2)] for i in range(3)]
         side = [
-            own_ref[i * 3, h] * shifted[i][0]
-            + own_ref[i * 3 + 1, h] * shifted[i][1]
-            + own_ref[i * 3 + 2, h] * shifted[i][2]
+            taps[h][i][0] * shifted[i][0]
+            + taps[h][i][1] * shifted[i][1]
+            + taps[h][i][2] * shifted[i][2]
             for i in range(3)
         ]
         xs.append(shifted)
@@ -251,18 +337,18 @@
         gated.append((side[1] * side[2]).astype(BF16))
         grad_mixed.append((x[3] * side[0]).astype(BF16))
     spec = forward_spectra(gated + grad_mixed, fwd_rows, cols, twist)
-    products = (
-        [times(spec[h], spec[2 + h], True) for h in range(2)]
-        + [times(spec[h], spec_ref[h], False) for h in range(2)]
-        + [times(spec_ref[h], spec[2 + h], True) for h in range(2)]
-    )
-    convs = inverse_spectra(products, back_cols, back_rows, twist)
+    pairs = [
+        [times(spec[h], spec[2 + h], True) for h in range(2)],
+        [times(spec[h], spec_ref[h], False) for h in range(2)],
+        [times(spec_ref[h], spec[2 + h], True) for h in range(2)],
+    ]
+    convs = inverse_pairs(pairs, back_cols, back_rows, twist)
 
     sums = []
     line_ref[...] = jnp.zeros_like(line_ref)
     for h in range(2):
         grad_filt = convs[h].astype(BF16).astype(F32)
-        window, slope = decay_window(own_ref, h)
+        window, slope = decay_window(rate_ref, rank, h)
         grad_raw = grad_filt * window
         sums.append(jnp.sum(grad_raw * raw_ref[h] * slope, axis=0, keepdims=True))
         for n in range(BLK):
@@ -270,10 +356,11 @@
 
     w2_hi, w2_lo = split(w2_ref[...])
     w2_stack = jnp.concatenate([w2_hi, w2_hi, w2_lo], axis=1)
-    col0 = wl_ref[:, 0:1]
-    col1 = wl_ref[:, 1:2]
-    shared = jnp.zeros((112, BLK), F32)
-    last = jnp.zeros((16, 64), F32)
+    col0 = picked(wl_ref[:, half(0)], rank)
+    col1 = picked(wl_ref[:, half(1)], rank)
+    total = jnp.zeros((BLK, 192), F32)
+    for move in moves:
+        move.wait()
     for j in range(line_ref.shape[1] // CHUNK):
         at = slice(j * CHUNK, (j + 1) * CHUNK)
         line = line_ref[:, at]
@@ -282,13 +369,14 @@
         grad_one = dot(w2_stack, jnp.concatenate([hi, lo, hi], axis=0)) * c1_ref[
             :, at
         ].astype(F32)
-        left = jnp.concatenate([a1_ref[:, at], feat_ref[0:48, at]], axis=0)
-        right = jnp.concatenate([hi, grad_one.astype(BF16)], axis=0)
-        shared = shared + dot_nt(left, right)
-        line_hi, line_lo = split(line)
-        last = last + dot_nt(jnp.concatenate([line_hi, line_lo], axis=0), a2_ref[:, at])
-
-    last = last[:8] + last[8:]
+        line_hi = line.astype(BF16).astype(F32)
+        lines = jnp.concatenate([line_hi, line - line_hi], axis=0).astype(BF16)
+        left = jnp.concatenate([a1_ref[:, at], feat_ref[:, at], lines], axis=0)
+        right = jnp.concatenate([hi, grad_one.astype(BF16), a2_ref[:, at]], axis=0)
+        total = total + dot_nt(left, right)
+
+    shared = total[:112, :BLK]
+    last = total[112:120, BLK:] + total[120:, BLK:]
     count = 33
     biases = shared[64 + ONES_ROW : 64 + ONES_ROW + 1]
     low = jnp.concatenate(
@@ -306,19 +394,18 @@
     back_ref[:, 9 * BLK :] = jnp.zeros((BLK, BLK), BF16)
 
     for h in range(2):
-        gain = own_ref[9, h]
         g = gated[h].astype(F32)
         gm = grad_mixed[h].astype(F32)
-        mixed = (convs[2 + h] + gain * g).astype(BF16).astype(F32)
-        grad_gated = (convs[4 + h] + gain * gm).astype(BF16).astype(F32)
+        mixed = (convs[2 + h] + gains[h] * g).astype(BF16).astype(F32)
+        grad_gated = (convs[4 + h] + gains[h] * gm).astype(BF16).astype(F32)
         side = sides[h]
         grad_side = [cots[h] * mixed, grad_gated * side[2], grad_gated * side[1]]
         back_ref[:, h * BLK : (h + 1) * BLK] = (side[0] * mixed).astype(BF16)
         sums.append(jnp.sum(gm * g, axis=0, keepdims=True))
         for i in range(3):
-            grad_stream = own_ref[i * 3, h] * grad_side[i]
+            grad_stream = taps[h][i][0] * grad_side[i]
             for m in range(1, 3):
-                grad_stream = grad_stream + own_ref[i * 3 + m, h] * later(grad_side[i], m)
+                grad_stream = grad_stream + taps[h][i][m] * later(grad_side[i], m)
             at = (2 + i * 2 + h) * BLK
             back_ref[:, at : at + BLK] = grad_stream.astype(BF16)
             for m in range(3):
@@ -331,20 +418,14 @@
 
 
 def unpack_kernel(recv_ref, out_ref, grad_ref):
-    ident = eye()
     for i in range(4):
         for h in range(2):
             at = (i * 2 + h) * BLK
-            turned = lax.dot_general(
-                recv_ref[:, at : at + BLK],
-                ident,
-                (((0,), (0,)), ((), ())),
-                preferred_element_type=F32,
-            ).astype(BF16)
+            block = turned(recv_ref[:, at : at + BLK]).astype(BF16)
             if i == 0:
-                out_ref[:, h * BLK : (h + 1) * BLK] = turned
+                out_ref[:, half(h)] = block
             else:
-                grad_ref[i - 1, :, h * BLK : (h + 1) * BLK] = turned
+                grad_ref[i - 1, :, half(h)] = block
 
 
 def final_kernel(
@@ -362,20 +443,15 @@
     wl_ref[:, BLK:] = high[:64]
     rest = high[64:]
     for h in range(2):
-        at = slice(h * BLK, (h + 1) * BLK)
-        rate_ref[:, at] = rest[h : h + 1]
-        skip_ref[:, at] = rest[2 + 10 * h : 3 + 10 * h]
-        taps_ref[:, at] = rest[3 + 10 * h : 12 + 10 * h]
+        rate_ref[:, half(h)] = rest[h : h + 1]
+        skip_ref[:, half(h)] = rest[2 + 10 * h : 3 + 10 * h]
+        for i in range(3):
+            at = 3 + 10 * h + 3 * i
+            taps_ref[i, :, half(h)] = rest[at : at + 3]
 
 
 def params(**kwargs):
     return pltpu.CompilerParams(vmem_limit_bytes=VMEM, **kwargs)
-
-
-def stacked_weights(weights, order):
-    hi = lax.reduce_precision(weights, 8, 7)
-    lo = weights - hi
-    return jnp.concatenate([lo if name == "lo" else hi for name in order], axis=0)
 
 
 def on_device(
@@ -400,44 +476,17 @@
     smem = pl.BlockSpec(memory_space=pltpu.SMEM)
     shape = jax.ShapeDtypeStruct
 
+    row = rank.reshape(1).astype(jnp.int32)
     outgoing = pl.pallas_call(
         pack_kernel,
-        out_shape=shape((peers, 8 * tok), BF16),
+        out_shape=shape((peers, 8, tok), BF16),
+        scratch_shapes=[pltpu.VMEM((peers, 8, tok), F32)],
         name="pack_rows",
     )(streams, cotangent)
-    incoming = lax.all_to_all(
-        outgoing.reshape(peers, 8, tok), "ctx", split_axis=0, concat_axis=0, tiled=True
-    ).reshape(peers, 8 * tok)
-
-    table = jnp.concatenate(
-        [short_taps.reshape(9, channels), skip_gain[None], decay_rate[None], w_last], axis=0
-    )
-    own = lax.dynamic_index_in_dim(
-        table.reshape(11 + hid, 2, peers), rank, axis=2, keepdims=False
-    )
-    own_wl = own[11:]
+    incoming = lax.all_to_all(outgoing, "ctx", split_axis=0, concat_axis=0, tiled=True)
+
     fwd_rows, cols, twist, back_cols, back_rows = (jnp.asarray(c) for c in dft_consts())
     feat = jnp.asarray(feature_const(seq_len, (count - 1) // 2))
-    b_hi = lax.reduce_precision(b_first, 8, 7)
-    w_hi = lax.reduce_precision(w_first, 8, 7)
-    w1 = (
-        jnp.concatenate(
-            [
-                w_hi,
-                b_hi[None],
-                (b_first - b_hi)[None],
-                jnp.zeros((LO_ROW - ONES_ROW - 2, hid), F32),
-                w_hi,
-                w_first - w_hi,
-                jnp.zeros((BLK - HI_ROW - count, hid), F32),
-            ],
-            axis=0,
-        )
-        .T.astype(BF16)
-    )
-    w2_hi = lax.reduce_precision(w_second, 8, 7)
-    w2 = jnp.concatenate([w2_hi, w2_hi, w_second - w2_hi], axis=0).T.astype(BF16)
-
     act = shape((hid, seq_len), BF16)
     act_spec = pl.BlockSpec((hid, CHUNK), lambda j: (0, j))
     whole = lambda *dims: pl.BlockSpec(dims, lambda j: (0,) * len(dims))
@@ -445,11 +494,13 @@
         net_kernel,
         grid=(seq_len // CHUNK,),
         in_specs=[
+            smem,
             pl.BlockSpec((BLK, CHUNK), lambda j: (0, j)),
-            whole(hid, BLK),
-            whole(hid, 3 * hid),
-            whole(hid, 1),
-            whole(hid, 2),
+            whole(count, hid),
+            whole(1, hid),
+            whole(hid, hid),
+            whole(1, hid),
+            whole(hid, channels),
         ],
         out_specs=[
             act_spec,
@@ -459,28 +510,47 @@
             pl.BlockSpec((2, CHUNK // BLK, BLK), lambda j: (0, j, 0)),
         ],
         out_shape=[act, act, act, act, shape((2, BLK, BLK), F32)],
+        scratch_shapes=[
+            pltpu.VMEM((hid, BLK), BF16),
+            pltpu.VMEM((hid, 3 * hid + 16), BF16),
+            pltpu.VMEM((hid, 2 * BLK), F32),
+        ],
         compiler_params=params(dimension_semantics=("arbitrary",)),
         name="filter_net",
-    )(feat, w1, w2, b_second[:, None], own_wl)
+    )(row, feat, w_first, b_first[None], w_second, b_second[None], w_last)
     filt_spec = pl.pallas_call(
         filt_kernel,
-        in_specs=[smem] + [vmem] * 4,
+        in_specs=[smem] + [vmem] * 5,
         out_specs=vmem,
         out_shape=shape((2, SIDE, SIDE), F32),
         compiler_params=params(),
         name="filter_spectrum",
-    )(own, raw, fwd_rows, cols, twist)
+    )(row, decay_rate[None], raw, fwd_rows, cols, twist)
 
     back, vec = pl.pallas_call(
         owner_kernel,
-        in_specs=[smem] + [vmem] * 15,
+        in_specs=[smem] + [vmem] * 13 + [pl.BlockSpec(memory_space=pl.ANY)] * 5,
         out_specs=[vmem, vmem],
         out_shape=[shape((peers, 10 * tok), BF16), shape((1, 2 * BLK), F32)],
-        scratch_shapes=[pltpu.VMEM((8, seq_len), F32)],
+        scratch_shapes=[
+            pltpu.VMEM((8, seq_len), F32),
+            pltpu.VMEM((peers, 8, tok), F32),
+            pltpu.VMEM((48, seq_len), BF16),
+            pltpu.VMEM((hid, seq_len), BF16),
+            pltpu.VMEM((hid, seq_len), BF16),
+            pltpu.VMEM((hid, seq_len), BF16),
+            pltpu.VMEM((hid, seq_len), BF16),
+            pltpu.SemaphoreType.DMA((5,)),
+        ],
         compiler_params=params(),
         name="convolve_channels",
     )(
-        own,
+        row,
+        short_taps,
+        skip_gain[None],
+        decay_rate[None],
+        w_second,
+        w_last,
         incoming,
         raw,
         filt_spec,
@@ -490,8 +560,6 @@
         back_cols,
         back_rows,
         feat,
-        w_second,
-        own_wl,
         a1,
         c1,
         a2,
@@ -500,6 +568,7 @@
     returned = lax.all_to_all(
         back.reshape(peers, 2, 5 * tok), "ctx", split_axis=0, concat_axis=0, tiled=True
     ).reshape(peers, 10 * tok)
+    returned, vec = lax.optimization_barrier((returned, vec))
     halves = jnp.sum(returned[:, 8 * tok : 9 * tok].astype(F32), axis=0)
     mine = lax.psum(halves[:64] + halves[64:], "tp")
     vec = jnp.concatenate([mine[None], vec[:, 64:]], axis=1)
@@ -513,7 +582,7 @@
     taps, gw1, gb1, gw2, gb2, gwl, rate, skip = pl.pallas_call(
         final_kernel,
         out_shape=[
-            shape((9, channels), F32),
+            shape((3, 3, channels), F32),
             shape((count, hid), F32),
             shape((1, hid), F32),
             shape((hid, hid), F32),
@@ -527,7 +596,7 @@
     return (
         output,
         grad_streams,
-        taps.reshape(3, 3, channels),
+        taps,
         gw1,
         gb1[0],
         gw2,

time: 147 us -> 130 us (0.88)
  blocking collectives: 7.14 us -> 41.4 us
  starting transfers between devices: 43.8 us -> 26.8 us
  waiting for transfers between devices: 40.8 us -> 24.2 us
  local copies, waits for them, and re-layouts: 15.5 us -> 3.95 us
  Pallas kernels: 36.2 us -> 31.9 us
  other arithmetic: 2.38 us -> 0.19 us
    all_to_all x0 -> x1, blocking collectives: none -> 34.2 us  [on_device(): lax.all_to_all(back.reshape(peers, 2, 5 * tok), 'ctx', split_axis=0, conc...]
    all_to_all x2 -> x1, starting transfers between devices: 37.7 us -> 20.6 us  [on_device(): lax.all_to_all(outgoing, 'ctx', split_axis=0, concat_axis=0, tiled=True)]
    all_to_all x2 -> x1, waiting for transfers between devices: 24.5 us -> 7.93 us  [on_device(): lax.all_to_all(outgoing, 'ctx', split_axis=0, concat_axis=0, tiled=True)]
    pallas_call x5, Pallas kernels: 34.3 us -> 30 us  [the longest x1 12.5 us: on_device(): pl.pallas_call(net_kernel, grid=(seq_len // CHUNK,), in_specs=[smem, pl.B...]
    unnamed x12 -> x6, local copies, waits for them, and re-layouts: 4.82 us -> 1.41 us
    concatenate x7 -> x0, local copies, waits for them, and re-layouts: 2.88 us -> none  [the longest x6 2.17 us: on_device(): jnp.concatenate([short_taps.reshape(9, channels), skip_gain[None], decay_...]
    broadcast_in_dim x5 -> x0, local copies, waits for them, and re-layouts: 1.6 us -> none  [the longest x1 1.36 us: on_device(): b_second[:, None]]
  transfers between devices with their start and end apart: 3 -> 2, of which waited for: 2 -> 2; matrix products, arithmetic and copies ran while one was open for 7% -> 0% of each run, Pallas kernels for 14% -> 13%
where the time goes in v2:
time: 130 us; the launch traced here: 129 us
  blocking collectives  41.4 us (32%)
  Pallas kernels  31.9 us (25%)
  starting transfers between devices  26.8 us (21%)
  waiting for transfers between devices  24.2 us (19%)
  local copies, waits for them, and re-layouts  3.95 us (3%)
    all_to_all x1, blocking collectives, on_device(): lax.all_to_all(back.reshape(peers, 2, 5 * tok), 'ctx', split_axis=0, conc...  34.2 us
    all_to_all x1, starting transfers between devices, on_device(): lax.all_to_all(outgoing, 'ctx', split_axis=0, concat_axis=0, tiled=True)  20.6 us
    all_to_all x1, waiting for transfers between devices, on_device(): lax.all_to_all(spread, 'ctx', split_axis=0, concat_axis=0, tiled=True)  16.3 us
    pallas_call x1, Pallas kernels, on_device(): pl.pallas_call(net_kernel, grid=(seq_len // CHUNK,), in_specs=[smem, pl.B...  12.5 us
    pallas_call x1, Pallas kernels, on_device(): pl.pallas_call(owner_kernel, in_specs=[smem] + [vmem] * 13 + [pl.BlockSpe...  10.8 us
    all_to_all x1, waiting for transfers between devices, on_device(): lax.all_to_all(outgoing, 'ctx', split_axis=0, concat_axis=0, tiled=True)  7.93 us
    psum x1, blocking collectives, on_device(): mine = lax.psum(halves[:64] + halves[64:], 'tp')  7.14 us
    all_to_all x1, starting transfers between devices, on_device(): lax.all_to_all(spread, 'ctx', split_axis=0, concat_axis=0, tiled=True)  6.19 us
  transfers between devices with their start and end apart: 2, of which 2 were waited for; matrix products, arithmetic and copies ran while one was open for 0% of the time, Pallas kernels for 13%

profile of v2, /device:TPU:4, one launch (start us, length us, event | category | flops | bytes accessed | tf_op | source)
XLA Modules:
  0.0 129.1 jit_solution(11740616797038375575)
XLA Ops:
  0.6 2.2 %pack_rows.1 = bf16[128,8,128]{2,1,0:T(8,128)(2,1)} custom-call(bf16[3,128,256]{2,1,0:T(8,128)(2,1)} %streams_ref.1, bf16[128,256]{1,0:T(8,128)(2,1)} %cot_ref.1), custom_call_target="tpu_custom_call" | custom-call | tf_op jit(solution)/shard_map/pack_rows/pallas_call | solution.py:480
  2.8 20.6 %all-to-all-start = ((bf16[128,8,128]{2,1,0:T(8,128)(2,1)}), bf16[128,8,128]{2,1,0:T(8,128)(2,1)S(1)}, u32[]{:S(2)}, u32[]{:S(2)}) async-start(bf16[128,8,128]{2,1,0:T(8,128)(2,1)} %pack_rows.1), calls=%async_computation | async-start | bytes 524288 | tf_op jit(solution)/shard_map/all_to_all | solution.py:486
  23.4 12.5 %filter_net.1 = (bf16[64,16384]{1,0:T(8,128)(2,1)}, bf16[64,16384]{1,0:T(8,128)(2,1)}, bf16[64,16384]{1,0:T(8,128)(2,1)}, bf16[64,16384]{1,0:T(8,128)(2,1)}, f32[2,128,128]{2,1,0:T(8,128)}) custom-call(s32[1]{0:T(128)} %bitcast.rank_ref, bf16[128,16384]{1,0:T(8,128)(2,1)} %constant.25.clone.feat_ref.feat_any, f32[33,64]{1,0:T(8,128)} %w1_ref.1, ...), custom_call_target="tpu_custom_call" | custom-call | tf_op jit(solution)/shard_map/filter_net/pallas_call | solution.py:493
  35.9 2.8 %filter_spectrum.1.spec_ref = f32[2,256,256]{2,1,0:T(8,128)} custom-call(s32[1]{0:T(128)} %bitcast.rank_ref, f32[1,256]{1,0:T(1,128)} %bitcast.21, f32[2,128,128]{2,1,0:T(8,128)} %get-tuple-element.29.raw_ref, bf16[512,256]{1,0:T(8,128)(2,1)} %constant.20.clone.fwd_rows, bf16[512,256]{1,0:T(8,128)(2,1)} %constant.21.clone.cols, f32[256,256]{1,0:T(8,128)} %constant.22.clone.twist), custom_call_target="tpu_custom_call" | custom-call | tf_op jit(solution)/shard_map/filter_spectrum/pallas_call | solution.py:521
  38.7 7.9 %all-to-all-done.recv_ref = bf16[128,8,128]{2,1,0:T(8,128)(2,1)S(1)} async-done(((bf16[128,8,128]{2,1,0:T(8,128)(2,1)}), bf16[128,8,128]{2,1,0:T(8,128)(2,1)S(1)}, u32[]{:S(2)}, u32[]{:S(2)}) %all-to-all-start) | async-done | bytes 262176 | tf_op jit(solution)/shard_map/all_to_all | solution.py:486
  46.6 0.0 copy-start.1
  46.6 0.7 copy-done.1
  47.4 10.8 %convolve_channels.1 = (bf16[128,1280]{1,0:T(8,128)(2,1)}, f32[1,256]{1,0:T(1,128)}) custom-call(s32[1]{0:T(128)} %bitcast.rank_ref, f32[3,3,256]{2,1,0:T(4,128)} %taps_ref.1, f32[1,256]{1,0:T(1,128)} %bitcast.24, f32[1,256]{1,0:T(1,128)} %bitcast.22, f32[64,64]{1,0:T(8,128)} %w2_ref.3, f32[64,256]{1,0:T(8,128)} %wl_ref.3, bf16[128,8,128]{2,1,0:T(8,128)(2,1)} %copy-done.1, ...), custom_call_target="tpu_custom_call" | custom-call | tf_op jit(solution)/shard_map/convolve_channels/pallas_call | solution.py:530
  58.2 1.1 reshape.36
  59.2 34.2 %all_to_all.18 = bf16[128,2,640]{2,1,0:T(2,128)(2,1)S(1)} all-to-all(bf16[128,2,640]{2,1,0:T(2,128)(2,1)S(1)} %reshape.36), channel_id=1, replica_groups=mesh['ctx'=128,'tp'=4] {'ctx'}, dimensions={0} | all-to-all | bytes 655360 | tf_op jit(solution)/shard_map/all_to_all | solution.py:568
  93.5 0.0 copy-start
  93.5 0.8 slice.15
  94.3 0.1 add_bitcast_fusion
  94.4 7.1 %psum.7 = f32[1,64]{1,0:T(1,128)S(1)} all-reduce(f32[1,64]{1,0:T(1,128)S(1)} %add_bitcast_fusion), channel_id=1, replica_groups=mesh['ctx'=128,'tp'=4] {'tp'}, use_global_device_ids=true, to_apply=%region_1.0 | all-reduce | flops 64 | bytes 512 | tf_op jit(solution)/shard_map/psum | solution.py:573
  101.5 0.1 pad_maximum_fusion
  101.6 0.7 broadcast_in_dim.26
  102.3 6.2 %all-to-all-start.2 = ((f32[128,1,256]{2,1,0:T(1,128)}), f32[128,1,256]{2,1,0:T(1,128)S(1)}, u32[]{:S(2)}, u32[]{:S(2)}) async-start(f32[128,1,256]{2,1,0:T(1,128)} %broadcast_in_dim.26), calls=%async_computation.2 | async-start | bytes 262144 | tf_op jit(solution)/shard_map/all_to_all | solution.py:576
  108.5 0.0 copy-done
  108.5 1.9 %unpack_rows.1 = (bf16[128,256]{1,0:T(8,128)(2,1)}, bf16[3,128,256]{2,1,0:T(8,128)(2,1)}) custom-call(bf16[128,1280]{1,0:T(8,128)(2,1)} %bitcast.18), custom_call_target="tpu_custom_call" | custom-call | tf_op jit(solution)/shard_map/unpack_rows/pallas_call | solution.py:577
  110.4 16.3 %all-to-all-done.2 = f32[128,1,256]{2,1,0:T(1,128)S(1)} async-done(((f32[128,1,256]{2,1,0:T(1,128)}), f32[128,1,256]{2,1,0:T(1,128)S(1)}, u32[]{:S(2)}, u32[]{:S(2)}) %all-to-all-start.2) | async-done | bytes 131104 | tf_op jit(solution)/shard_map/all_to_all | solution.py:576
  126.8 0.7 copy.29
  127.4 1.7 %unpack_sums.1 = (f32[3,3,256]{2,1,0:T(4,128)}, f32[33,64]{1,0:T(8,128)}, f32[1,64]{1,0:T(1,128)}, f32[64,64]{1,0:T(8,128)}, f32[1,64]{1,0:T(1,128)}, /*index=5*...) custom-call(f32[128,256]{1,0:T(8,128)} %bitcast.20), custom_call_target="tpu_custom_call" | custom-call | tf_op jit(solution)/shard_map/unpack_sums/pallas_call | solution.py:582
  (2 shorter events, 0.1 us)
Async XLA Ops:
  2.8 43.8 %all-to-all-start = ((bf16[128,8,128]{2,1,0:T(8,128)(2,1)}), bf16[128,8,128]{2,1,0:T(8,128)(2,1)S(1)}, u32[]{:S(2)}, u32[]{:S(2)}) async-start(bf16[128,8,128]{2,1,0:T(8,128)(2,1)} %pack_rows.1), calls=%async_computation | async-start | bytes 524288 | tf_op jit(solution)/shard_map/all_to_all | solution.py:486
  46.6 0.7 copy-start.1
  93.5 15.0 %copy-start = (bf16[16,8,2,640]{3,1,2,0:T(8,128)(2,1)}, bf16[16,8,2,640]{3,1,2,0:T(8,128)(2,1)S(1)}, u32[]{:S(2)}) copy-start(bf16[16,8,2,640]{3,1,2,0:T(8,128)(2,1)S(1)} %copy.27) | copy-start | bytes 983044
  102.3 24.4 %all-to-all-start.2 = ((f32[128,1,256]{2,1,0:T(1,128)}), f32[128,1,256]{2,1,0:T(1,128)S(1)}, u32[]{:S(2)}, u32[]{:S(2)}) async-start(f32[128,1,256]{2,1,0:T(1,128)} %broadcast_in_dim.26), calls=%async_computation.2 | async-start | bytes 262144 | tf_op jit(solution)/shard_map/all_to_all | solution.py:576

commit v3 on v2

--- a/solution.py
+++ b/solution.py
@@ -17,6 +17,8 @@
 ONES_ROW = 33
 LO_ROW = 36
 HI_ROW = 69
+AHEAD_HI = 16
+AHEAD_LO = 32
 VMEM = 56 * 1024 * 1024
 NT = (((1,), (1,)), ((), ()))
 
@@ -390,9 +392,10 @@
     )
     packed = jnp.concatenate([shared[:64, :64], low], axis=1).T
     p_hi, p_lo = split(packed)
-    back_ref[:, 8 * BLK : 9 * BLK] = jnp.concatenate([p_hi, p_lo], axis=1)
-    back_ref[:, 9 * BLK :] = jnp.zeros((BLK, BLK), BF16)
-
+    back_ref[:, 4 * BLK : 5 * BLK] = jnp.concatenate([p_hi, p_lo], axis=1)
+
+    lane = places()[1]
+    edge = jnp.zeros((BLK, BLK), F32)
     for h in range(2):
         g = gated[h].astype(F32)
         gm = grad_mixed[h].astype(F32)
@@ -400,16 +403,23 @@
         grad_gated = (convs[4 + h] + gains[h] * gm).astype(BF16).astype(F32)
         side = sides[h]
         grad_side = [cots[h] * mixed, grad_gated * side[2], grad_gated * side[1]]
-        back_ref[:, h * BLK : (h + 1) * BLK] = (side[0] * mixed).astype(BF16)
+        back_ref[:, half(h)] = mixed.astype(BF16)
+        back_ref[:, half(2 + h)] = grad_gated.astype(BF16)
         sums.append(jnp.sum(gm * g, axis=0, keepdims=True))
         for i in range(3):
-            grad_stream = taps[h][i][0] * grad_side[i]
-            for m in range(1, 3):
-                grad_stream = grad_stream + taps[h][i][m] * later(grad_side[i], m)
-            at = (2 + i * 2 + h) * BLK
-            back_ref[:, at : at + BLK] = grad_stream.astype(BF16)
+            at = 2 * (i * 2 + h)
+            before = jnp.where(lane < 2, xs[h][i][2], 0.0)
+            after = jnp.where(lane >= BLK - 2, later(grad_side[i], 2), 0.0)
+            after_hi = after.astype(BF16).astype(F32)
+            edge = (
+                edge
+                + pltpu.roll(before, at, 1)
+                + pltpu.roll(after_hi, AHEAD_HI + 2 + at, 1)
+                + pltpu.roll(after - after_hi, AHEAD_LO + 2 + at, 1)
+            )
             for m in range(3):
                 sums.append(jnp.sum(grad_side[i] * xs[h][i][m], axis=0, keepdims=True))
+    back_ref[:, 5 * BLK :] = edge.astype(BF16)
     sums = jnp.concatenate(sums + [jnp.zeros((64 - len(sums), BLK), F32)], axis=0)
     totals = dot_nt(jnp.ones((8, BLK), F32), sums, lax.Precision.HIGHEST)
     vec_ref[...] = jnp.concatenate(
@@ -417,15 +427,45 @@
     )
 
 
-def unpack_kernel(recv_ref, out_ref, grad_ref):
-    for i in range(4):
-        for h in range(2):
-            at = (i * 2 + h) * BLK
-            block = turned(recv_ref[:, at : at + BLK]).astype(BF16)
-            if i == 0:
-                out_ref[:, half(h)] = block
-            else:
-                grad_ref[i - 1, :, half(h)] = block
+def rows_kernel(recv_ref, streams_ref, cot_ref, taps_ref, out_ref, grad_ref):
+    row = places()[0]
+    edge = turned(recv_ref[:, 5 * BLK :])
+    for h in range(2):
+        mixed = turned(recv_ref[:, half(h)])
+        grad_gated = turned(recv_ref[:, half(2 + h)])
+        side = []
+        for i in range(3):
+            at = 2 * (i * 2 + h)
+            x = streams_ref[i, :, half(h)].astype(F32)
+            far, near = edge[at : at + 1], edge[at + 1 : at + 2]
+            one = jnp.where(row == 0, near, pltpu.roll(x, 1, 0))
+            two = jnp.where(row == 0, far, jnp.where(row == 1, near, pltpu.roll(x, 2, 0)))
+            side.append(
+                taps_ref[i, 0:1, half(h)] * x
+                + taps_ref[i, 1:2, half(h)] * one
+                + taps_ref[i, 2:3, half(h)] * two
+            )
+        out_ref[:, half(h)] = (side[0] * mixed).astype(BF16)
+        cot = cot_ref[:, half(h)].astype(F32)
+        grad_side = [cot * mixed, grad_gated * side[2], grad_gated * side[1]]
+        for i in range(3):
+            at = 2 * (i * 2 + h)
+            ahead = (
+                edge[AHEAD_HI + at : AHEAD_HI + at + 2] + edge[AHEAD_LO + at : AHEAD_LO + at + 2]
+            )
+            near, far = ahead[0:1], ahead[1:2]
+            g = grad_side[i]
+            one = jnp.where(row == BLK - 1, near, pltpu.roll(g, BLK - 1, 0))
+            two = jnp.where(
+                row == BLK - 1,
+                far,
+                jnp.where(row == BLK - 2, near, pltpu.roll(g, BLK - 2, 0)),
+            )
+            grad_ref[i, :, half(h)] = (
+                taps_ref[i, 0:1, half(h)] * g
+                + taps_ref[i, 1:2, half(h)] * one
+                + taps_ref[i, 2:3, half(h)] * two
+            ).astype(BF16)
 
 
 def final_kernel(
@@ -531,7 +571,7 @@
         owner_kernel,
         in_specs=[smem] + [vmem] * 13 + [pl.BlockSpec(memory_space=pl.ANY)] * 5,
         out_specs=[vmem, vmem],
-        out_shape=[shape((peers, 10 * tok), BF16), shape((1, 2 * BLK), F32)],
+        out_shape=[shape((peers, 6 * tok), BF16), shape((1, 2 * BLK), F32)],
         scratch_shapes=[
             pltpu.VMEM((8, seq_len), F32),
             pltpu.VMEM((peers, 8, tok), F32),
@@ -566,19 +606,20 @@
         c2,
     )
     returned = lax.all_to_all(
-        back.reshape(peers, 2, 5 * tok), "ctx", split_axis=0, concat_axis=0, tiled=True
-    ).reshape(peers, 10 * tok)
+        back.reshape(peers, 2, 3 * tok), "ctx", split_axis=0, concat_axis=0, tiled=True
+    ).reshape(peers, 6 * tok)
     returned, vec = lax.optimization_barrier((returned, vec))
-    halves = jnp.sum(returned[:, 8 * tok : 9 * tok].astype(F32), axis=0)
+    halves = jnp.sum(returned[:, 4 * tok : 5 * tok].astype(F32), axis=0)
     mine = lax.psum(halves[:64] + halves[64:], "tp")
     vec = jnp.concatenate([mine[None], vec[:, 64:]], axis=1)
     spread = jnp.broadcast_to(vec, (peers, 2 * BLK))
     gathered = lax.all_to_all(spread, "ctx", split_axis=0, concat_axis=0, tiled=True)
     output, grad_streams = pl.pallas_call(
-        unpack_kernel,
+        rows_kernel,
         out_shape=[shape((tok, channels), BF16), shape((3, tok, channels), BF16)],
-        name="unpack_rows",
-    )(returned)
+        compiler_params=params(),
+        name="finish_rows",
+    )(returned, streams, cotangent, short_taps)
     taps, gw1, gb1, gw2, gb2, gwl, rate, skip = pl.pallas_call(
         final_kernel,
         out_shape=[

time: 130 us -> 124 us (0.954)
  blocking collectives: 41.4 us -> 36.2 us
    all_to_all x1, blocking collectives: 34.2 us -> 29.1 us  [on_device(): lax.all_to_all(back.reshape(peers, 2, 3 * tok), 'ctx', split_axis=0, conc...]
  transfers between devices with their start and end apart: 2 -> 2, of which waited for: 2 -> 2; matrix products, arithmetic and copies ran while one was open for 0% -> 0% of each run, Pallas kernels for 13% -> 14%
where the time goes in v3:
time: 124 us
  blocking collectives  36.2 us (29%)
  Pallas kernels  32.1 us (26%)
  starting transfers between devices  26.7 us (22%)
  waiting for transfers between devices  24 us (19%)
  local copies, waits for them, and re-layouts  3.9 us (3%)
    all_to_all x1, blocking collectives, on_device(): lax.all_to_all(back.reshape(peers, 2, 3 * tok), 'ctx', split_axis=0, conc...  29.1 us
    all_to_all x1, starting transfers between devices, on_device(): lax.all_to_all(outgoing, 'ctx', split_axis=0, concat_axis=0, tiled=True)  20.6 us
    all_to_all x1, waiting for transfers between devices, on_device(): lax.all_to_all(spread, 'ctx', split_axis=0, concat_axis=0, tiled=True)  16.1 us
    pallas_call x1, Pallas kernels, on_device(): pl.pallas_call(net_kernel, grid=(seq_len // CHUNK,), in_specs=[smem, pl.B...  12.5 us
    pallas_call x1, Pallas kernels, on_device(): pl.pallas_call(owner_kernel, in_specs=[smem] + [vmem] * 13 + [pl.BlockSpe...  10.7 us
    all_to_all x1, waiting for transfers between devices, on_device(): lax.all_to_all(outgoing, 'ctx', split_axis=0, concat_axis=0, tiled=True)  7.9 us
    psum x1, blocking collectives, on_device(): mine = lax.psum(halves[:64] + halves[64:], 'tp')  7.14 us
    all_to_all x1, starting transfers between devices, on_device(): lax.all_to_all(spread, 'ctx', split_axis=0, concat_axis=0, tiled=True)  6.16 us
  transfers between devices with their start and end apart: 2, of which 2 were waited for; matrix products, arithmetic and copies ran while one was open for 0% of the time, Pallas kernels for 14%

profile of v3, /device:TPU:4, one launch (start us, length us, event | category | flops | bytes accessed | tf_op | source)
XLA Modules:
  0.0 123.9 jit_solution(11468346311624680998)
XLA Ops:
  0.6 2.2 %pack_rows.1 = bf16[128,8,128]{2,1,0:T(8,128)(2,1)} custom-call(bf16[3,128,256]{2,1,0:T(8,128)(2,1)} %streams_ref.3, bf16[128,256]{1,0:T(8,128)(2,1)} %cot_ref.3), custom_call_target="tpu_custom_call" | custom-call | tf_op jit(solution)/shard_map/pack_rows/pallas_call | solution.py:520
  2.8 20.6 %all-to-all-start = ((bf16[128,8,128]{2,1,0:T(8,128)(2,1)}), bf16[128,8,128]{2,1,0:T(8,128)(2,1)S(1)}, u32[]{:S(2)}, u32[]{:S(2)}) async-start(bf16[128,8,128]{2,1,0:T(8,128)(2,1)} %pack_rows.1), calls=%async_computation | async-start | bytes 524288 | tf_op jit(solution)/shard_map/all_to_all | solution.py:526
  23.4 12.5 %filter_net.1 = (bf16[64,16384]{1,0:T(8,128)(2,1)}, bf16[64,16384]{1,0:T(8,128)(2,1)}, bf16[64,16384]{1,0:T(8,128)(2,1)}, bf16[64,16384]{1,0:T(8,128)(2,1)}, f32[2,128,128]{2,1,0:T(8,128)}) custom-call(s32[1]{0:T(128)} %bitcast.rank_ref, bf16[128,16384]{1,0:T(8,128)(2,1)} %constant.25.clone.feat_ref.feat_any, f32[33,64]{1,0:T(8,128)} %w1_ref.1, ...), custom_call_target="tpu_custom_call" | custom-call | tf_op jit(solution)/shard_map/filter_net/pallas_call | solution.py:533
  36.0 2.8 %filter_spectrum.1.spec_ref = f32[2,256,256]{2,1,0:T(8,128)} custom-call(s32[1]{0:T(128)} %bitcast.rank_ref, f32[1,256]{1,0:T(1,128)} %bitcast.21, f32[2,128,128]{2,1,0:T(8,128)} %get-tuple-element.29.raw_ref, bf16[512,256]{1,0:T(8,128)(2,1)} %constant.20.clone.fwd_rows, bf16[512,256]{1,0:T(8,128)(2,1)} %constant.21.clone.cols, f32[256,256]{1,0:T(8,128)} %constant.22.clone.twist), custom_call_target="tpu_custom_call" | custom-call | tf_op jit(solution)/shard_map/filter_spectrum/pallas_call | solution.py:561
  38.7 7.9 %all-to-all-done.recv_ref = bf16[128,8,128]{2,1,0:T(8,128)(2,1)S(1)} async-done(((bf16[128,8,128]{2,1,0:T(8,128)(2,1)}), bf16[128,8,128]{2,1,0:T(8,128)(2,1)S(1)}, u32[]{:S(2)}, u32[]{:S(2)}) %all-to-all-start) | async-done | bytes 262176 | tf_op jit(solution)/shard_map/all_to_all | solution.py:526
  46.6 0.0 copy-start
  46.6 0.7 copy-done
  47.4 10.7 %convolve_channels.1 = (bf16[128,768]{1,0:T(8,128)(2,1)}, f32[1,256]{1,0:T(1,128)}) custom-call(s32[1]{0:T(128)} %bitcast.rank_ref, f32[3,3,256]{2,1,0:T(4,128)} %taps_ref.3, f32[1,256]{1,0:T(1,128)} %bitcast.24, f32[1,256]{1,0:T(1,128)} %bitcast.22, f32[64,64]{1,0:T(8,128)} %w2_ref.3, f32[64,256]{1,0:T(8,128)} %wl_ref.3, bf16[128,8,128]{2,1,0:T(8,128)(2,1)} %copy-done, ...), custom_call_target="tpu_custom_call" | custom-call | tf_op jit(solution)/shard_map/convolve_channels/pallas_call | solution.py:570
  58.1 1.0 reshape.36
  59.1 29.1 %all_to_all.18 = bf16[128,2,384]{2,1,0:T(2,128)(2,1)S(1)} all-to-all(bf16[128,2,384]{2,1,0:T(2,128)(2,1)S(1)} %reshape.36), channel_id=1, replica_groups=mesh['ctx'=128,'tp'=4] {'ctx'}, dimensions={0} | all-to-all | bytes 393216 | tf_op jit(solution)/shard_map/all_to_all | solution.py:608
  88.2 0.0 copy-start.1
  88.2 0.8 slice.15
  89.0 0.1 add_bitcast_fusion
  89.1 7.1 %psum.7 = f32[1,64]{1,0:T(1,128)S(1)} all-reduce(f32[1,64]{1,0:T(1,128)S(1)} %add_bitcast_fusion), channel_id=1, replica_groups=mesh['ctx'=128,'tp'=4] {'tp'}, use_global_device_ids=true, to_apply=%region_1.0 | all-reduce | flops 64 | bytes 512 | tf_op jit(solution)/shard_map/psum | solution.py:613
  96.2 0.1 pad_maximum_fusion
  96.3 0.7 broadcast_in_dim.26
  97.0 6.2 %all-to-all-start.2 = ((f32[128,1,256]{2,1,0:T(1,128)}), f32[128,1,256]{2,1,0:T(1,128)S(1)}, u32[]{:S(2)}, u32[]{:S(2)}) async-start(f32[128,1,256]{2,1,0:T(1,128)} %broadcast_in_dim.26), calls=%async_computation.2 | async-start | bytes 262144 | tf_op jit(solution)/shard_map/all_to_all | solution.py:616
  103.2 0.0 copy-done.1
  103.2 2.2 %finish_rows.1 = (bf16[128,256]{1,0:T(8,128)(2,1)}, bf16[3,128,256]{2,1,0:T(8,128)(2,1)}) custom-call(bf16[128,768]{1,0:T(8,128)(2,1)} %bitcast.18, bf16[3,128,256]{2,1,0:T(8,128)(2,1)} %streams_ref.3, bf16[128,256]{1,0:T(8,128)(2,1)} %cot_ref.3, f32[3,3,256]{2,1,0:T(4,128)} %taps_ref.3), custom_call_target="tpu_custom_call" | custom-call | tf_op jit(solution)/shard_map/finish_rows/pallas_call | solution.py:617
  105.4 16.1 %all-to-all-done.2 = f32[128,1,256]{2,1,0:T(1,128)S(1)} async-done(((f32[128,1,256]{2,1,0:T(1,128)}), f32[128,1,256]{2,1,0:T(1,128)S(1)}, u32[]{:S(2)}, u32[]{:S(2)}) %all-to-all-start.2) | async-done | bytes 131104 | tf_op jit(solution)/shard_map/all_to_all | solution.py:616
  121.5 0.7 copy.29
  122.2 1.7 %unpack_sums.1 = (f32[3,3,256]{2,1,0:T(4,128)}, f32[33,64]{1,0:T(8,128)}, f32[1,64]{1,0:T(1,128)}, f32[64,64]{1,0:T(8,128)}, f32[1,64]{1,0:T(1,128)}, /*index=5*...) custom-call(f32[128,256]{1,0:T(8,128)} %bitcast.20), custom_call_target="tpu_custom_call" | custom-call | tf_op jit(solution)/shard_map/unpack_sums/pallas_call | solution.py:623
  (2 shorter events, 0.1 us)
Async XLA Ops:
  2.8 43.8 %all-to-all-start = ((bf16[128,8,128]{2,1,0:T(8,128)(2,1)}), bf16[128,8,128]{2,1,0:T(8,128)(2,1)S(1)}, u32[]{:S(2)}, u32[]{:S(2)}) async-start(bf16[128,8,128]{2,1,0:T(8,128)(2,1)} %pack_rows.1), calls=%async_computation | async-start | bytes 524288 | tf_op jit(solution)/shard_map/all_to_all | solution.py:526
  46.6 0.7 copy-start
  88.2 15.0 %copy-start.1 = (bf16[16,8,2,384]{3,1,2,0:T(8,128)(2,1)}, bf16[16,8,2,384]{3,1,2,0:T(8,128)(2,1)S(1)}, u32[]{:S(2)}) copy-start(bf16[16,8,2,384]{3,1,2,0:T(8,128)(2,1)S(1)} %copy.27) | copy-start | bytes 589828
  97.0 24.5 %all-to-all-start.2 = ((f32[128,1,256]{2,1,0:T(1,128)}), f32[128,1,256]{2,1,0:T(1,128)S(1)}, u32[]{:S(2)}, u32[]{:S(2)}) async-start(f32[128,1,256]{2,1,0:T(1,128)} %broadcast_in_dim.26), calls=%async_computation.2 | async-start | bytes 262144 | tf_op jit(solution)/shard_map/all_to_all | solution.py:616

commit v4 on v3

--- a/solution.py
+++ b/solution.py
@@ -68,7 +68,7 @@
     r = np.cos(np.linspace(0.0, np.pi / 2, 4001))[:-1]
     powers = np.stack([r ** (2 * i) for i in range(6)], 1)
     s = np.linalg.lstsq(powers * r[:, None], np.sin(np.pi * r), rcond=None)[0]
-    c = np.linalg.lstsq(powers, np.cos(np.pi * r), rcond=None)[0]
+    c = np.linalg.lstsq(powers[:, :5], np.cos(np.pi * r), rcond=None)[0]
     return [float(v) for v in s], [float(v) for v in c]
 
 
@@ -78,9 +78,9 @@
 def sin_cos_pi(x):
     r = x - 2.0 * jnp.round(x * 0.5)
     z = r * r
-    s = SIN_C[5] * z + SIN_C[4]
-    c = COS_C[5] * z + COS_C[4]
-    for i in range(3, -1, -1):
+    s = (SIN_C[5] * z + SIN_C[4]) * z + SIN_C[3]
+    c = COS_C[4] * z + COS_C[3]
+    for i in range(2, -1, -1):
         s = s * z + SIN_C[i]
         c = c * z + COS_C[i]
     return s * r, c
@@ -212,17 +212,37 @@
     w2_ref,
     b2_ref,
     wl_ref,
-    a1_ref,
+    rate_ref,
+    rows_any,
+    cols_any,
+    twist_any,
+    lt_ref,
     c1_ref,
     a2_ref,
     c2_ref,
     raw_ref,
+    spec_ref,
     w1_hold,
     w2_hold,
     wl_hold,
+    fwd_rows,
+    cols,
+    twist,
+    sems,
 ):
-    @pl.when(pl.program_id(0) == 0)
+    step = pl.program_id(0)
+    moves = [
+        pltpu.make_async_copy(src, dst, sems.at[k])
+        for k, (src, dst) in enumerate(
+            [(rows_any, fwd_rows), (cols_any, cols), (twist_any, twist)]
+        )
+    ]
+
+    @pl.when(step == 0)
     def _():
+        for move in moves:
+            move.start()
+
         def parts(ref):
             x = ref[...] * (1.0 / math.pi)
             hi = x.astype(BF16).astype(F32)
@@ -247,9 +267,9 @@
             )
 
     one, cos_one = sin_cos_pi(dot(w1_hold[...], feat_ref[...]))
-    a1_ref[...] = one.astype(BF16)
     c1_ref[...] = cos_one.astype(BF16)
     hi, lo = split(one)
+    lt_ref[...] = jnp.concatenate([hi, feat_ref[0:64, :]], axis=0).T
     ones = jnp.ones((16, CHUNK), BF16)
     two, cos_two = sin_cos_pi(dot(w2_hold[...], jnp.concatenate([hi, lo, hi, ones], axis=0)))
     a2_ref[...] = two.astype(BF16)
@@ -258,16 +278,19 @@
         col = wl_hold[:, h * BLK : h * BLK + 1]
         row = jnp.sum(col * two, axis=0, keepdims=True)
         for j in range(CHUNK // BLK):
-            raw_ref[h, j : j + 1, :] = row[:, j * BLK : (j + 1) * BLK]
-
-
-def filt_kernel(rank_ref, rate_ref, raw_ref, fwd_rows, cols, twist, spec_ref):
-    signals = [
-        (raw_ref[h] * decay_window(rate_ref, rank_ref[0], h)[0]).astype(BF16)
-        for h in range(2)
-    ]
-    for h, spec in enumerate(forward_spectra(signals, fwd_rows, cols, twist)):
-        spec_ref[h] = spec
+            at = step * (CHUNK // BLK) + j
+            raw_ref[h, pl.ds(at, 1), :] = row[:, j * BLK : (j + 1) * BLK]
+
+    @pl.when(step == pl.num_programs(0) - 1)
+    def _():
+        signals = [
+            (raw_ref[h] * decay_window(rate_ref, rank_ref[0], h)[0]).astype(BF16)
+            for h in range(2)
+        ]
+        for move in moves:
+            move.wait()
+        for h, spec in enumerate(forward_spectra(signals, fwd_rows, cols, twist)):
+            spec_ref[h] = spec
 
 
 def owner_kernel(
@@ -278,40 +301,15 @@
     w2_ref,
     wl_ref,
     recv_ref,
-    raw_ref,
-    spec_ref,
-    fwd_rows,
-    cols,
-    twist,
-    back_cols,
-    back_rows,
-    feat_any,
-    a1_any,
-    c1_any,
-    a2_any,
-    c2_any,
-    back_ref,
-    vec_ref,
-    line_ref,
-    hold_ref,
-    feat_ref,
-    a1_ref,
-    c1_ref,
-    a2_ref,
-    c2_ref,
-    sems,
+    *refs,
 ):
+    large, back_ref, vec_ref, line_ref, hold_ref = refs[:11], *refs[11:15]
+    copies, sems = refs[15:26], refs[26]
+    fwd_rows, cols, twist, back_cols, back_rows, spec_ref, raw_ref = copies[:7]
+    c2_ref, c1_ref, lt_ref, a2_ref = copies[7:]
     moves = [
         pltpu.make_async_copy(src, dst, sems.at[k])
-        for k, (src, dst) in enumerate(
-            [
-                (c2_any, c2_ref),
-                (c1_any, c1_ref),
-                (a1_any, a1_ref),
-                (feat_any.at[pl.ds(0, 48), :], feat_ref),
-                (a2_any, a2_ref),
-            ]
-        )
+        for k, (src, dst) in enumerate(zip(large, copies))
     ]
     for move in moves:
         move.start()
@@ -338,6 +336,8 @@
         cots.append(x[3])
         gated.append((side[1] * side[2]).astype(BF16))
         grad_mixed.append((x[3] * side[0]).astype(BF16))
+    for move in moves[:7]:
+        move.wait()
     spec = forward_spectra(gated + grad_mixed, fwd_rows, cols, twist)
     pairs = [
         [times(spec[h], spec[2 + h], True) for h in range(2)],
@@ -357,40 +357,41 @@
             line_ref[h : h + 1, n * BLK : (n + 1) * BLK] = grad_raw[n : n + 1, :]
 
     w2_hi, w2_lo = split(w2_ref[...])
-    w2_stack = jnp.concatenate([w2_hi, w2_hi, w2_lo], axis=1)
+    w2_stack = jnp.concatenate([w2_hi, w2_lo], axis=1)
     col0 = picked(wl_ref[:, half(0)], rank)
     col1 = picked(wl_ref[:, half(1)], rank)
-    total = jnp.zeros((BLK, 192), F32)
-    for move in moves:
+    total = jnp.zeros((BLK, BLK), F32)
+    last = jnp.zeros((64, 16), F32)
+    for move in moves[7:]:
         move.wait()
     for j in range(line_ref.shape[1] // CHUNK):
         at = slice(j * CHUNK, (j + 1) * CHUNK)
         line = line_ref[:, at]
         grad_two = (col0 * line[0:1] + col1 * line[1:2]) * c2_ref[:, at].astype(F32)
-        hi, lo = split(grad_two)
-        grad_one = dot(w2_stack, jnp.concatenate([hi, lo, hi], axis=0)) * c1_ref[
+        hi = grad_two.astype(BF16)
+        grad_one = dot(w2_stack, jnp.concatenate([hi, hi], axis=0)) * c1_ref[
             :, at
         ].astype(F32)
         line_hi = line.astype(BF16).astype(F32)
         lines = jnp.concatenate([line_hi, line - line_hi], axis=0).astype(BF16)
-        left = jnp.concatenate([a1_ref[:, at], feat_ref[:, at], lines], axis=0)
-        right = jnp.concatenate([hi, grad_one.astype(BF16), a2_ref[:, at]], axis=0)
-        total = total + dot_nt(left, right)
-
-    shared = total[:112, :BLK]
-    last = total[112:120, BLK:] + total[120:, BLK:]
+        right = jnp.concatenate([hi, grad_one.astype(BF16)], axis=0)
+        total = total + dot(right, lt_ref[at, :])
+        last = last + dot_nt(a2_ref[:, at], lines)
+
+    last = jnp.concatenate([last, jnp.zeros((64, BLK - 16), F32)], axis=1).T
+    last = last[:8] + last[8:16]
     count = 33
-    biases = shared[64 + ONES_ROW : 64 + ONES_ROW + 1]
+    bias_at = slice(64 + ONES_ROW, 65 + ONES_ROW)
     low = jnp.concatenate(
         [
-            shared[64 : 64 + count, 64:],
-            biases[:, 64:],
-            biases[:, :64],
-            jnp.zeros((64 - count - 2, 64), F32),
+            total[64:, 64 : 64 + count],
+            total[64:, bias_at],
+            total[:64, bias_at],
+            jnp.zeros((64, 64 - count - 2), F32),
         ],
-        axis=0,
-    )
-    packed = jnp.concatenate([shared[:64, :64], low], axis=1).T
+        axis=1,
+    )
+    packed = jnp.concatenate([total[:64, :64], low], axis=0)
     p_hi, p_lo = split(packed)
     back_ref[:, 4 * BLK : 5 * BLK] = jnp.concatenate([p_hi, p_lo], axis=1)
 
@@ -471,8 +472,8 @@
 def final_kernel(
     all_ref, taps_ref, w1_ref, b1_ref, w2_ref, b2_ref, wl_ref, rate_ref, skip_ref
 ):
-    low = all_ref[:, :BLK].T
-    high = all_ref[:, BLK:].T
+    low = all_ref[:, 0, :BLK].T
+    high = all_ref[:, 0, BLK:].T
     shared = low[:64]
     flipped = shared[:, 64:]
     w2_ref[...] = shared[:, :64]
@@ -514,6 +515,7 @@
     count, hid = w_first.shape
     vmem = pl.BlockSpec(memory_space=pltpu.VMEM)
     smem = pl.BlockSpec(memory_space=pltpu.SMEM)
+    far = pl.BlockSpec(memory_space=pl.ANY)
     shape = jax.ShapeDtypeStruct
 
     row = rank.reshape(1).astype(jnp.int32)
@@ -530,7 +532,7 @@
     act = shape((hid, seq_len), BF16)
     act_spec = pl.BlockSpec((hid, CHUNK), lambda j: (0, j))
     whole = lambda *dims: pl.BlockSpec(dims, lambda j: (0,) * len(dims))
-    a1, c1, a2, c2, raw = pl.pallas_call(
+    lt, c1, a2, c2, raw, filt_spec = pl.pallas_call(
         net_kernel,
         grid=(seq_len // CHUNK,),
         in_specs=[
@@ -541,46 +543,56 @@
             whole(hid, hid),
             whole(1, hid),
             whole(hid, channels),
+            whole(1, channels),
+            far,
+            far,
+            far,
         ],
         out_specs=[
+            pl.BlockSpec((CHUNK, BLK), lambda j: (j, 0)),
             act_spec,
             act_spec,
             act_spec,
-            act_spec,
-            pl.BlockSpec((2, CHUNK // BLK, BLK), lambda j: (0, j, 0)),
+            whole(2, BLK, BLK),
+            whole(2, SIDE, SIDE),
         ],
-        out_shape=[act, act, act, act, shape((2, BLK, BLK), F32)],
+        out_shape=[shape((seq_len, BLK), BF16), act, act, act, shape((2, BLK, BLK), F32), shape((2, SIDE, SIDE), F32)],
         scratch_shapes=[
             pltpu.VMEM((hid, BLK), BF16),
             pltpu.VMEM((hid, 3 * hid + 16), BF16),
             pltpu.VMEM((hid, 2 * BLK), F32),
+            pltpu.VMEM(fwd_rows.shape, BF16),
+            pltpu.VMEM(cols.shape, BF16),
+            pltpu.VMEM(twist.shape, F32),
+            pltpu.SemaphoreType.DMA((3,)),
         ],
         compiler_params=params(dimension_semantics=("arbitrary",)),
         name="filter_net",
-    )(row, feat, w_first, b_first[None], w_second, b_second[None], w_last)
-    filt_spec = pl.pallas_call(
-        filt_kernel,
-        in_specs=[smem] + [vmem] * 5,
-        out_specs=vmem,
-        out_shape=shape((2, SIDE, SIDE), F32),
-        compiler_params=params(),
-        name="filter_spectrum",
-    )(row, decay_rate[None], raw, fwd_rows, cols, twist)
-
+    )(
+        row,
+        feat,
+        w_first,
+        b_first[None],
+        w_second,
+        b_second[None],
+        w_last,
+        decay_rate[None],
+        fwd_rows,
+        cols,
+        twist,
+    )
+
+    large = [fwd_rows, cols, twist, back_cols, back_rows, filt_spec, raw, c2, c1, lt, a2]
     back, vec = pl.pallas_call(
         owner_kernel,
-        in_specs=[smem] + [vmem] * 13 + [pl.BlockSpec(memory_space=pl.ANY)] * 5,
+        in_specs=[smem] + [vmem] * 6 + [far] * 11,
         out_specs=[vmem, vmem],
         out_shape=[shape((peers, 6 * tok), BF16), shape((1, 2 * BLK), F32)],
         scratch_shapes=[
             pltpu.VMEM((8, seq_len), F32),
             pltpu.VMEM((peers, 8, tok), F32),
-            pltpu.VMEM((48, seq_len), BF16),
-            pltpu.VMEM((hid, seq_len), BF16),
-            pltpu.VMEM((hid, seq_len), BF16),
-            pltpu.VMEM((hid, seq_len), BF16),
-            pltpu.VMEM((hid, seq_len), BF16),
-            pltpu.SemaphoreType.DMA((5,)),
+            *[pltpu.VMEM(x.shape, x.dtype) for x in large],
+            pltpu.SemaphoreType.DMA((len(large),)),
         ],
         compiler_params=params(),
         name="convolve_channels",
@@ -592,18 +604,7 @@
         w_second,
         w_last,
         incoming,
-        raw,
-        filt_spec,
-        fwd_rows,
-        cols,
-        twist,
-        back_cols,
-        back_rows,
-        feat,
-        a1,
-        c1,
-        a2,
-        c2,
+        *large,
     )
     returned = lax.all_to_all(
         back.reshape(peers, 2, 3 * tok), "ctx", split_axis=0, concat_axis=0, tiled=True
@@ -612,7 +613,7 @@
     halves = jnp.sum(returned[:, 4 * tok : 5 * tok].astype(F32), axis=0)
     mine = lax.psum(halves[:64] + halves[64:], "tp")
     vec = jnp.concatenate([mine[None], vec[:, 64:]], axis=1)
-    spread = jnp.broadcast_to(vec, (peers, 2 * BLK))
+    spread = jnp.broadcast_to(vec[None], (peers, 1, 2 * BLK))
     gathered = lax.all_to_all(spread, "ctx", split_axis=0, concat_axis=0, tiled=True)
     output, grad_streams = pl.pallas_call(
         rows_kernel,

time: 124 us -> 122 us (0.984)
  Pallas kernels: 32.1 us -> 29.6 us
    pallas_call x2 -> x1, Pallas kernels: 13.5 us -> 9.48 us  [on_device(): pl.pallas_call(owner_kernel, in_specs=[smem] + [vmem] * 6 + [far] * 11, o...]
    pallas_call x1, Pallas kernels: 12.5 us -> 14.1 us  [on_device(): pl.pallas_call(net_kernel, grid=(seq_len // CHUNK,), in_specs=[smem, pl.B...]
  transfers between devices with their start and end apart: 2 -> 2, of which waited for: 2 -> 2; matrix products, arithmetic and copies ran while one was open for 0% -> 0% of each run, Pallas kernels for 14% -> 13%
where the time goes in v4:
time: 122 us
  blocking collectives  35.5 us (29%)
  Pallas kernels  29.6 us (24%)
  starting transfers between devices  26.7 us (22%)
  waiting for transfers between devices  25 us (20%)
  local copies, waits for them, and re-layouts  3.86 us (3%)
    all_to_all x1, blocking collectives, on_device(): lax.all_to_all(back.reshape(peers, 2, 3 * tok), 'ctx', split_axis=0, conc...  28.1 us
    all_to_all x1, starting transfers between devices, on_device(): lax.all_to_all(outgoing, 'ctx', split_axis=0, concat_axis=0, tiled=True)  20.6 us
    all_to_all x1, waiting for transfers between devices, on_device(): lax.all_to_all(spread, 'ctx', split_axis=0, concat_axis=0, tiled=True)  16.1 us
    pallas_call x1, Pallas kernels, on_device(): pl.pallas_call(net_kernel, grid=(seq_len // CHUNK,), in_specs=[smem, pl.B...  14.1 us
    pallas_call x1, Pallas kernels, on_device(): pl.pallas_call(owner_kernel, in_specs=[smem] + [vmem] * 6 + [far] * 11, o...  9.48 us
    all_to_all x1, waiting for transfers between devices, on_device(): lax.all_to_all(outgoing, 'ctx', split_axis=0, concat_axis=0, tiled=True)  8.82 us
    psum x1, blocking collectives, on_device(): mine = lax.psum(halves[:64] + halves[64:], 'tp')  7.32 us
    all_to_all x1, starting transfers between devices, on_device(): lax.all_to_all(spread, 'ctx', split_axis=0, concat_axis=0, tiled=True)  6.15 us
  transfers between devices with their start and end apart: 2, of which 2 were waited for; matrix products, arithmetic and copies ran while one was open for 0% of the time, Pallas kernels for 13%

profile of v4, /device:TPU:4, one launch (start us, length us, event | category | flops | bytes accessed | tf_op | source)
XLA Modules:
  0.0 121.5 jit_solution(16519118685220156498)
XLA Ops:
  0.6 2.1 %pack_rows.1 = bf16[128,8,128]{2,1,0:T(8,128)(2,1)} custom-call(bf16[3,128,256]{2,1,0:T(8,128)(2,1)} %streams_ref.3, bf16[128,256]{1,0:T(8,128)(2,1)} %cot_ref.3), custom_call_target="tpu_custom_call" | custom-call | tf_op jit(solution)/shard_map/pack_rows/pallas_call | solution.py:522
  2.8 20.6 %all-to-all-start = ((bf16[128,8,128]{2,1,0:T(8,128)(2,1)}), bf16[128,8,128]{2,1,0:T(8,128)(2,1)S(1)}, u32[]{:S(2)}, u32[]{:S(2)}) async-start(bf16[128,8,128]{2,1,0:T(8,128)(2,1)} %pack_rows.1), calls=%async_computation | async-start | bytes 524288 | tf_op jit(solution)/shard_map/all_to_all | solution.py:528
  23.4 14.1 %filter_net.1 = (bf16[16384,128]{1,0:T(8,128)(2,1)}, bf16[64,16384]{1,0:T(8,128)(2,1)}, bf16[64,16384]{1,0:T(8,128)(2,1)}, bf16[64,16384]{1,0:T(8,128)(2,1)}, f3...) custom-call(s32[1]{0:T(128)} %bitcast.rank_ref, bf16[128,16384]{1,0:T(8,128)(2,1)} %constant.25.clone.feat_ref, ...), custom_call_target="tpu_custom_call" | custom-call | tf_op jit(solution)/shard_map/filter_net/pallas_call | solution.py:535
  37.5 8.8 %all-to-all-done.recv_ref = bf16[128,8,128]{2,1,0:T(8,128)(2,1)S(1)} async-done(((bf16[128,8,128]{2,1,0:T(8,128)(2,1)}), bf16[128,8,128]{2,1,0:T(8,128)(2,1)S(1)}, u32[]{:S(2)}, u32[]{:S(2)}) %all-to-all-start) | async-done | bytes 262176 | tf_op jit(solution)/shard_map/all_to_all | solution.py:528
  46.3 0.0 copy-start
  46.3 0.7 copy-done
  47.0 9.5 %convolve_channels.1 = (bf16[128,768]{1,0:T(8,128)(2,1)}, f32[1,256]{1,0:T(1,128)}) custom-call(s32[1]{0:T(128)} %bitcast.rank_ref, f32[3,3,256]{2,1,0:T(4,128)} %taps_ref.3, f32[1,256]{1,0:T(1,128)} %bitcast.20, f32[1,256]{1,0:T(1,128)} %bitcast.19, f32[64,64]{1,0:T(8,128)} %w2_ref.3, f32[64,256]{1,0:T(8,128)} %wl_ref.3, bf16[128,8,128]{2,1,0:T(8,128)(2,1)} %copy-done, ...), custom_call_target="tpu_custom_call" | custom-call | tf_op jit(solution)/shard_map/convolve_channels/pallas_call | solution.py:586
  56.5 1.0 reshape.33
  57.5 28.1 %all_to_all.15 = bf16[128,2,384]{2,1,0:T(2,128)(2,1)S(1)} all-to-all(bf16[128,2,384]{2,1,0:T(2,128)(2,1)S(1)} %reshape.33), channel_id=1, replica_groups=mesh['ctx'=128,'tp'=4] {'ctx'}, dimensions={0} | all-to-all | bytes 393216 | tf_op jit(solution)/shard_map/all_to_all | solution.py:609
  85.7 0.0 copy-start.1
  85.7 0.8 slice.15
  86.5 0.1 add_bitcast_fusion
  86.6 7.3 %psum.7 = f32[1,64]{1,0:T(1,128)S(1)} all-reduce(f32[1,64]{1,0:T(1,128)S(1)} %add_bitcast_fusion), channel_id=1, replica_groups=mesh['ctx'=128,'tp'=4] {'tp'}, use_global_device_ids=true, to_apply=%region_1.0 | all-reduce | flops 64 | bytes 512 | tf_op jit(solution)/shard_map/psum | solution.py:614
  93.9 0.1 pad_maximum_fusion
  94.0 0.7 broadcast_in_dim.30
  94.7 6.2 %all-to-all-start.2 = ((f32[128,1,256]{2,1,0:T(1,128)}), f32[128,1,256]{2,1,0:T(1,128)S(1)}, u32[]{:S(2)}, u32[]{:S(2)}) async-start(f32[128,1,256]{2,1,0:T(1,128)} %broadcast_in_dim.30), calls=%async_computation.2 | async-start | bytes 262144 | tf_op jit(solution)/shard_map/all_to_all | solution.py:617
  100.9 0.0 copy-done.1
  100.9 2.2 %finish_rows.1 = (bf16[128,256]{1,0:T(8,128)(2,1)}, bf16[3,128,256]{2,1,0:T(8,128)(2,1)}) custom-call(bf16[128,768]{1,0:T(8,128)(2,1)} %bitcast.15, bf16[3,128,256]{2,1,0:T(8,128)(2,1)} %streams_ref.3, bf16[128,256]{1,0:T(8,128)(2,1)} %cot_ref.3, f32[3,3,256]{2,1,0:T(4,128)} %taps_ref.3), custom_call_target="tpu_custom_call" | custom-call | tf_op jit(solution)/shard_map/finish_rows/pallas_call | solution.py:618
  103.0 16.1 %all-to-all-done.2.all_ref = f32[128,1,256]{2,1,0:T(1,128)S(1)} async-done(((f32[128,1,256]{2,1,0:T(1,128)}), f32[128,1,256]{2,1,0:T(1,128)S(1)}, u32[]{:S(2)}, u32[]{:S(2)}) %all-to-all-start.2) | async-done | bytes 131104 | tf_op jit(solution)/shard_map/all_to_all | solution.py:617
  119.2 0.0 copy-start.2
  119.2 0.6 copy-done.2
  119.8 1.7 %unpack_sums.1 = (f32[3,3,256]{2,1,0:T(4,128)}, f32[33,64]{1,0:T(8,128)}, f32[1,64]{1,0:T(1,128)}, f32[64,64]{1,0:T(8,128)}, f32[1,64]{1,0:T(1,128)}, /*index=5*...) custom-call(f32[128,1,256]{2,1,0:T(1,128)} %copy-done.2), custom_call_target="tpu_custom_call" | custom-call | tf_op jit(solution)/shard_map/unpack_sums/pallas_call | solution.py:624
  (2 shorter events, 0.1 us)
Async XLA Ops:
  2.8 43.5 %all-to-all-start = ((bf16[128,8,128]{2,1,0:T(8,128)(2,1)}), bf16[128,8,128]{2,1,0:T(8,128)(2,1)S(1)}, u32[]{:S(2)}, u32[]{:S(2)}) async-start(bf16[128,8,128]{2,1,0:T(8,128)(2,1)} %pack_rows.1), calls=%async_computation | async-start | bytes 524288 | tf_op jit(solution)/shard_map/all_to_all | solution.py:528
  46.3 0.7 copy-start
  85.7 15.2 %copy-start.1 = (bf16[16,8,2,384]{3,1,2,0:T(8,128)(2,1)}, bf16[16,8,2,384]{3,1,2,0:T(8,128)(2,1)S(1)}, u32[]{:S(2)}) copy-start(bf16[16,8,2,384]{3,1,2,0:T(8,128)(2,1)S(1)} %copy.26) | copy-start | bytes 589828
  94.7 24.5 %all-to-all-start.2 = ((f32[128,1,256]{2,1,0:T(1,128)}), f32[128,1,256]{2,1,0:T(1,128)S(1)}, u32[]{:S(2)}, u32[]{:S(2)}) async-start(f32[128,1,256]{2,1,0:T(1,128)} %broadcast_in_dim.30), calls=%async_computation.2 | async-start | bytes 262144 | tf_op jit(solution)/shard_map/all_to_all | solution.py:617
  119.2 0.6 copy-start.2

commit v5 on v4

--- a/solution.py
+++ b/solution.py
@@ -14,6 +14,7 @@
 BLK = 128
 SIDE = 256
 CHUNK = 2048
+NET_CHUNK = 4096
 ONES_ROW = 33
 LO_ROW = 36
 HI_ROW = 69
@@ -67,7 +68,7 @@
 def fit_sin_cos():
     r = np.cos(np.linspace(0.0, np.pi / 2, 4001))[:-1]
     powers = np.stack([r ** (2 * i) for i in range(6)], 1)
-    s = np.linalg.lstsq(powers * r[:, None], np.sin(np.pi * r), rcond=None)[0]
+    s = np.linalg.lstsq(powers[:, :5] * r[:, None], np.sin(np.pi * r), rcond=None)[0]
     c = np.linalg.lstsq(powers[:, :5], np.cos(np.pi * r), rcond=None)[0]
     return [float(v) for v in s], [float(v) for v in c]
 
@@ -78,7 +79,7 @@
 def sin_cos_pi(x):
     r = x - 2.0 * jnp.round(x * 0.5)
     z = r * r
-    s = (SIN_C[5] * z + SIN_C[4]) * z + SIN_C[3]
+    s = SIN_C[4] * z + SIN_C[3]
     c = COS_C[4] * z + COS_C[3]
     for i in range(2, -1, -1):
         s = s * z + SIN_C[i]
@@ -270,15 +271,15 @@
     c1_ref[...] = cos_one.astype(BF16)
     hi, lo = split(one)
     lt_ref[...] = jnp.concatenate([hi, feat_ref[0:64, :]], axis=0).T
-    ones = jnp.ones((16, CHUNK), BF16)
+    ones = jnp.ones((16, NET_CHUNK), BF16)
     two, cos_two = sin_cos_pi(dot(w2_hold[...], jnp.concatenate([hi, lo, hi, ones], axis=0)))
     a2_ref[...] = two.astype(BF16)
     c2_ref[...] = cos_two.astype(BF16)
     for h in range(2):
         col = wl_hold[:, h * BLK : h * BLK + 1]
         row = jnp.sum(col * two, axis=0, keepdims=True)
-        for j in range(CHUNK // BLK):
-            at = step * (CHUNK // BLK) + j
+        for j in range(NET_CHUNK // BLK):
+            at = step * (NET_CHUNK // BLK) + j
             raw_ref[h, pl.ds(at, 1), :] = row[:, j * BLK : (j + 1) * BLK]
 
     @pl.when(step == pl.num_programs(0) - 1)
@@ -393,7 +394,8 @@
     )
     packed = jnp.concatenate([total[:64, :64], low], axis=0)
     p_hi, p_lo = split(packed)
-    back_ref[:, 4 * BLK : 5 * BLK] = jnp.concatenate([p_hi, p_lo], axis=1)
+    rows = [None] * 6
+    rows[4] = jnp.concatenate([p_hi, p_lo], axis=1)
 
     lane = places()[1]
     edge = jnp.zeros((BLK, BLK), F32)
@@ -404,8 +406,8 @@
         grad_gated = (convs[4 + h] + gains[h] * gm).astype(BF16).astype(F32)
         side = sides[h]
         grad_side = [cots[h] * mixed, grad_gated * side[2], grad_gated * side[1]]
-        back_ref[:, half(h)] = mixed.astype(BF16)
-        back_ref[:, half(2 + h)] = grad_gated.astype(BF16)
+        rows[h] = mixed
+        rows[2 + h] = grad_gated
         sums.append(jnp.sum(gm * g, axis=0, keepdims=True))
         for i in range(3):
             at = 2 * (i * 2 + h)
@@ -420,7 +422,10 @@
             )
             for m in range(3):
                 sums.append(jnp.sum(grad_side[i] * xs[h][i][m], axis=0, keepdims=True))
-    back_ref[:, 5 * BLK :] = edge.astype(BF16)
+    rows[5] = edge
+    for k in range(3):
+        pair = [rows[k].astype(F32), rows[3 + k].astype(F32)]
+        back_ref[:, :, half(k)] = jnp.stack(pair, axis=1).astype(BF16)
     sums = jnp.concatenate(sums + [jnp.zeros((64 - len(sums), BLK), F32)], axis=0)
     totals = dot_nt(jnp.ones((8, BLK), F32), sums, lax.Precision.HIGHEST)
     vec_ref[...] = jnp.concatenate(
@@ -530,14 +535,14 @@
     fwd_rows, cols, twist, back_cols, back_rows = (jnp.asarray(c) for c in dft_consts())
     feat = jnp.asarray(feature_const(seq_len, (count - 1) // 2))
     act = shape((hid, seq_len), BF16)
-    act_spec = pl.BlockSpec((hid, CHUNK), lambda j: (0, j))
+    act_spec = pl.BlockSpec((hid, NET_CHUNK), lambda j: (0, j))
     whole = lambda *dims: pl.BlockSpec(dims, lambda j: (0,) * len(dims))
     lt, c1, a2, c2, raw, filt_spec = pl.pallas_call(
         net_kernel,
-        grid=(seq_len // CHUNK,),
+        grid=(seq_len // NET_CHUNK,),
         in_specs=[
             smem,
-            pl.BlockSpec((BLK, CHUNK), lambda j: (0, j)),
+            pl.BlockSpec((BLK, NET_CHUNK), lambda j: (0, j)),
             whole(count, hid),
             whole(1, hid),
             whole(hid, hid),
@@ -549,7 +554,7 @@
             far,
         ],
         out_specs=[
-            pl.BlockSpec((CHUNK, BLK), lambda j: (j, 0)),
+            pl.BlockSpec((NET_CHUNK, BLK), lambda j: (j, 0)),
             act_spec,
             act_spec,
             act_spec,
@@ -587,7 +592,7 @@
         owner_kernel,
         in_specs=[smem] + [vmem] * 6 + [far] * 11,
         out_specs=[vmem, vmem],
-        out_shape=[shape((peers, 6 * tok), BF16), shape((1, 2 * BLK), F32)],
+        out_shape=[shape((peers, 2, 3 * tok), BF16), shape((1, 2 * BLK), F32)],
         scratch_shapes=[
             pltpu.VMEM((8, seq_len), F32),
             pltpu.VMEM((peers, 8, tok), F32),
@@ -606,11 +611,10 @@
         incoming,
         *large,
     )
-    returned = lax.all_to_all(
-        back.reshape(peers, 2, 3 * tok), "ctx", split_axis=0, concat_axis=0, tiled=True
-    ).reshape(peers, 6 * tok)
+    returned = lax.all_to_all(back, "ctx", split_axis=0, concat_axis=0, tiled=True)
     returned, vec = lax.optimization_barrier((returned, vec))
-    halves = jnp.sum(returned[:, 4 * tok : 5 * tok].astype(F32), axis=0)
+    halves = jnp.sum(returned[:, 1, tok : 2 * tok].astype(F32), axis=0)
+    returned = returned.reshape(peers, 6 * tok)
     mine = lax.psum(halves[:64] + halves[64:], "tp")
     vec = jnp.concatenate([mine[None], vec[:, 64:]], axis=1)
     spread = jnp.broadcast_to(vec[None], (peers, 1, 2 * BLK))

time: 122 us -> 120 us (0.984)
  blocking collectives: 35.5 us -> 34.1 us
    all_to_all x1, waiting for transfers between devices: 8.82 us -> 10.2 us  [on_device(): lax.all_to_all(outgoing, 'ctx', split_axis=0, concat_axis=0, tiled=True)]
  transfers between devices with their start and end apart: 2 -> 2, of which waited for: 2 -> 2; matrix products, arithmetic and copies ran while one was open for 0% -> 1% of each run, Pallas kernels for 13% -> 13%
where the time goes in v5:
time: 120 us
  blocking collectives  34.1 us (28%)
  Pallas kernels  28.6 us (24%)
  starting transfers between devices  26.7 us (22%)
  waiting for transfers between devices  25.7 us (21%)
  local copies, waits for them, and re-layouts  3.54 us (3%)
    all_to_all x1, blocking collectives, on_device(): lax.all_to_all(back, 'ctx', split_axis=0, concat_axis=0, tiled=True)  27 us
    all_to_all x1, starting transfers between devices, on_device(): lax.all_to_all(outgoing, 'ctx', split_axis=0, concat_axis=0, tiled=True)  20.6 us
    all_to_all x1, waiting for transfers between devices, on_device(): lax.all_to_all(spread, 'ctx', split_axis=0, concat_axis=0, tiled=True)  15.5 us
    pallas_call x1, Pallas kernels, on_device(): pl.pallas_call(net_kernel, grid=(seq_len // NET_CHUNK,), in_specs=[smem,...  13 us
    all_to_all x1, waiting for transfers between devices, on_device(): lax.all_to_all(outgoing, 'ctx', split_axis=0, concat_axis=0, tiled=True)  10.2 us
    pallas_call x1, Pallas kernels, on_device(): pl.pallas_call(owner_kernel, in_specs=[smem] + [vmem] * 6 + [far] * 11, o...  9.62 us
    psum x1, blocking collectives, on_device(): mine = lax.psum(halves[:64] + halves[64:], 'tp')  7.14 us
    all_to_all x1, starting transfers between devices, on_device(): lax.all_to_all(spread, 'ctx', split_axis=0, concat_axis=0, tiled=True)  6.16 us
  transfers between devices with their start and end apart: 2, of which 2 were waited for; matrix products, arithmetic and copies ran while one was open for 1% of the time, Pallas kernels for 13%

profile of v5, /device:TPU:4, one launch (start us, length us, event | category | flops | bytes accessed | tf_op | source)
XLA Modules:
  0.0 119.7 jit_solution(12828318379210860445)
XLA Ops:
  0.6 2.2 %pack_rows.1 = bf16[128,8,128]{2,1,0:T(8,128)(2,1)} custom-call(bf16[3,128,256]{2,1,0:T(8,128)(2,1)} %streams_ref.3, bf16[128,256]{1,0:T(8,128)(2,1)} %cot_ref.3), custom_call_target="tpu_custom_call" | custom-call | tf_op jit(solution)/shard_map/pack_rows/pallas_call | solution.py:527
  2.8 20.6 %all-to-all-start = ((bf16[128,8,128]{2,1,0:T(8,128)(2,1)}), bf16[128,8,128]{2,1,0:T(8,128)(2,1)S(1)}, u32[]{:S(2)}, u32[]{:S(2)}) async-start(bf16[128,8,128]{2,1,0:T(8,128)(2,1)} %pack_rows.1), calls=%async_computation | async-start | bytes 524288 | tf_op jit(solution)/shard_map/all_to_all | solution.py:533
  23.4 13.0 %filter_net.1 = (bf16[16384,128]{1,0:T(8,128)(2,1)}, bf16[64,16384]{1,0:T(8,128)(2,1)}, bf16[64,16384]{1,0:T(8,128)(2,1)}, bf16[64,16384]{1,0:T(8,128)(2,1)}, f3...) custom-call(s32[1]{0:T(128)} %bitcast.rank_ref, bf16[128,16384]{1,0:T(8,128)(2,1)} %constant.25.clone.feat_ref, ...), custom_call_target="tpu_custom_call" | custom-call | tf_op jit(solution)/shard_map/filter_net/pallas_call | solution.py:540
  36.4 10.2 %all-to-all-done.recv_ref = bf16[128,8,128]{2,1,0:T(8,128)(2,1)S(1)} async-done(((bf16[128,8,128]{2,1,0:T(8,128)(2,1)}), bf16[128,8,128]{2,1,0:T(8,128)(2,1)S(1)}, u32[]{:S(2)}, u32[]{:S(2)}) %all-to-all-start) | async-done | bytes 262176 | tf_op jit(solution)/shard_map/all_to_all | solution.py:533
  46.6 0.0 copy-start
  46.6 0.7 copy-done
  47.3 9.6 %convolve_channels.1 = (bf16[128,2,384]{2,1,0:T(2,128)(2,1)}, f32[1,256]{1,0:T(1,128)}) custom-call(s32[1]{0:T(128)} %bitcast.rank_ref, f32[3,3,256]{2,1,0:T(4,128)} %taps_ref.3, f32[1,256]{1,0:T(1,128)} %bitcast.19, f32[1,256]{1,0:T(1,128)} %bitcast.18, f32[64,64]{1,0:T(8,128)} %w2_ref.3, f32[64,256]{1,0:T(8,128)} %wl_ref.3, bf16[128,8,128]{2,1,0:T(8,128)(2,1)} %copy-done, ...), custom_call_target="tpu_custom_call" | custom-call | tf_op jit(solution)/shard_map/convolve_channels/pallas_call | solution.py:591
  57.0 27.0 %all_to_all.15 = bf16[128,2,384]{2,1,0:T(2,128)(2,1)S(1)} all-to-all(bf16[128,2,384]{2,1,0:T(2,128)(2,1)} %get-tuple-element.36), channel_id=1, replica_groups=mesh['ctx'=128,'tp'=4] {'ctx'}, dimensions={0} | all-to-all | bytes 393216 | tf_op jit(solution)/shard_map/all_to_all | solution.py:614
  83.9 0.8 slice.15
  84.7 0.2 convert_reduce_fusion
  84.8 0.1 add_bitcast_fusion
  84.9 7.1 %psum.7 = f32[1,64]{1,0:T(1,128)S(1)} all-reduce(f32[1,64]{1,0:T(1,128)S(1)} %add_bitcast_fusion), channel_id=1, replica_groups=mesh['ctx'=128,'tp'=4] {'tp'}, use_global_device_ids=true, to_apply=%region_1.0 | all-reduce | flops 64 | bytes 512 | tf_op jit(solution)/shard_map/psum | solution.py:618
  92.1 0.1 pad_maximum_fusion
  92.1 0.7 broadcast_in_dim.30
  92.9 6.2 %all-to-all-start.2 = ((f32[128,1,256]{2,1,0:T(1,128)}), f32[128,1,256]{2,1,0:T(1,128)S(1)}, u32[]{:S(2)}, u32[]{:S(2)}) async-start(f32[128,1,256]{2,1,0:T(1,128)} %broadcast_in_dim.30), calls=%async_computation.2 | async-start | bytes 262144 | tf_op jit(solution)/shard_map/all_to_all | solution.py:621
  99.0 0.7 copy.26
  99.7 2.2 %finish_rows.1 = (bf16[128,256]{1,0:T(8,128)(2,1)}, bf16[3,128,256]{2,1,0:T(8,128)(2,1)}) custom-call(bf16[128,768]{1,0:T(8,128)(2,1)} %bitcast.15, bf16[3,128,256]{2,1,0:T(8,128)(2,1)} %streams_ref.3, bf16[128,256]{1,0:T(8,128)(2,1)} %cot_ref.3, f32[3,3,256]{2,1,0:T(4,128)} %taps_ref.3), custom_call_target="tpu_custom_call" | custom-call | tf_op jit(solution)/shard_map/finish_rows/pallas_call | solution.py:622
  101.9 15.5 %all-to-all-done.2.all_ref = f32[128,1,256]{2,1,0:T(1,128)S(1)} async-done(((f32[128,1,256]{2,1,0:T(1,128)}), f32[128,1,256]{2,1,0:T(1,128)S(1)}, u32[]{:S(2)}, u32[]{:S(2)}) %all-to-all-start.2) | async-done | bytes 131104 | tf_op jit(solution)/shard_map/all_to_all | solution.py:621
  117.3 0.0 copy-start.1
  117.3 0.7 copy-done.1
  118.0 1.7 %unpack_sums.1 = (f32[3,3,256]{2,1,0:T(4,128)}, f32[33,64]{1,0:T(8,128)}, f32[1,64]{1,0:T(1,128)}, f32[64,64]{1,0:T(8,128)}, f32[1,64]{1,0:T(1,128)}, /*index=5*...) custom-call(f32[128,1,256]{2,1,0:T(1,128)} %copy-done.1), custom_call_target="tpu_custom_call" | custom-call | tf_op jit(solution)/shard_map/unpack_sums/pallas_call | solution.py:628
Async XLA Ops:
  2.8 43.8 %all-to-all-start = ((bf16[128,8,128]{2,1,0:T(8,128)(2,1)}), bf16[128,8,128]{2,1,0:T(8,128)(2,1)S(1)}, u32[]{:S(2)}, u32[]{:S(2)}) async-start(bf16[128,8,128]{2,1,0:T(8,128)(2,1)} %pack_rows.1), calls=%async_computation | async-start | bytes 524288 | tf_op jit(solution)/shard_map/all_to_all | solution.py:533
  46.6 0.7 copy-start
  92.9 24.5 %all-to-all-start.2 = ((f32[128,1,256]{2,1,0:T(1,128)}), f32[128,1,256]{2,1,0:T(1,128)S(1)}, u32[]{:S(2)}, u32[]{:S(2)}) async-start(f32[128,1,256]{2,1,0:T(1,128)} %broadcast_in_dim.30), calls=%async_computation.2 | async-start | bytes 262144 | tf_op jit(solution)/shard_map/all_to_all | solution.py:621
  117.3 0.7 copy-start.1

commit v6 on v5

--- a/solution.py
+++ b/solution.py
@@ -306,16 +306,22 @@
 ):
     large, back_ref, vec_ref, line_ref, hold_ref = refs[:11], *refs[11:15]
     copies, sems = refs[15:26], refs[26]
+    got_ref, got_sem = refs[27:]
+    got = pltpu.make_async_copy(recv_ref, got_ref, got_sem)
+    got.start()
     fwd_rows, cols, twist, back_cols, back_rows, spec_ref, raw_ref = copies[:7]
     c2_ref, c1_ref, lt_ref, a2_ref = copies[7:]
     moves = [
         pltpu.make_async_copy(src, dst, sems.at[k])
         for k, (src, dst) in enumerate(zip(large, copies))
     ]
-    for move in moves:
+    for move in moves[:7]:
         move.start()
     rank = rank_ref[0]
-    hold_ref[...] = recv_ref[...].astype(F32)
+    got.wait()
+    for move in moves[7:]:
+        move.start()
+    hold_ref[...] = got_ref[...].astype(F32)
     taps, gains = [], []
     xs, sides, cots, gated, grad_mixed = [], [], [], [], []
     for h in range(2):
@@ -475,8 +481,21 @@
 
 
 def final_kernel(
-    all_ref, taps_ref, w1_ref, b1_ref, w2_ref, b2_ref, wl_ref, rate_ref, skip_ref
+    far_ref,
+    taps_ref,
+    w1_ref,
+    b1_ref,
+    w2_ref,
+    b2_ref,
+    wl_ref,
+    rate_ref,
+    skip_ref,
+    all_ref,
+    sem,
 ):
+    move = pltpu.make_async_copy(far_ref, all_ref, sem)
+    move.start()
+    move.wait()
     low = all_ref[:, 0, :BLK].T
     high = all_ref[:, 0, BLK:].T
     shared = low[:64]
@@ -590,7 +609,7 @@
     large = [fwd_rows, cols, twist, back_cols, back_rows, filt_spec, raw, c2, c1, lt, a2]
     back, vec = pl.pallas_call(
         owner_kernel,
-        in_specs=[smem] + [vmem] * 6 + [far] * 11,
+        in_specs=[smem] + [vmem] * 5 + [far] * 12,
         out_specs=[vmem, vmem],
         out_shape=[shape((peers, 2, 3 * tok), BF16), shape((1, 2 * BLK), F32)],
         scratch_shapes=[
@@ -598,6 +617,8 @@
             pltpu.VMEM((peers, 8, tok), F32),
             *[pltpu.VMEM(x.shape, x.dtype) for x in large],
             pltpu.SemaphoreType.DMA((len(large),)),
+            pltpu.VMEM((peers, 8, tok), BF16),
+            pltpu.SemaphoreType.DMA,
         ],
         compiler_params=params(),
         name="convolve_channels",
@@ -627,6 +648,8 @@
     )(returned, streams, cotangent, short_taps)
     taps, gw1, gb1, gw2, gb2, gwl, rate, skip = pl.pallas_call(
         final_kernel,
+        in_specs=[far],
+        scratch_shapes=[pltpu.VMEM((peers, 1, 2 * BLK), F32), pltpu.SemaphoreType.DMA],
         out_shape=[
             shape((3, 3, channels), F32),
             shape((count, hid), F32),

time: 120 us -> 121 us (level)
  no operation moved by 1% of the time
where the time goes in v6:
time: 121 us
  blocking collectives  34.1 us (28%)
  Pallas kernels  29.4 us (24%)
  starting transfers between devices  26.7 us (22%)
  waiting for transfers between devices  25.7 us (21%)
  local copies, waits for them, and re-layouts  3.54 us (3%)
    all_to_all x1, blocking collectives, on_device(): lax.all_to_all(back, 'ctx', split_axis=0, concat_axis=0, tiled=True)  27 us
    all_to_all x1, starting transfers between devices, on_device(): lax.all_to_all(outgoing, 'ctx', split_axis=0, concat_axis=0, tiled=True)  20.6 us
    all_to_all x1, waiting for transfers between devices, on_device(): lax.all_to_all(spread, 'ctx', split_axis=0, concat_axis=0, tiled=True)  15.5 us
    pallas_call x1, Pallas kernels, on_device(): pl.pallas_call(net_kernel, grid=(seq_len // NET_CHUNK,), in_specs=[smem,...  13 us
    pallas_call x1, Pallas kernels, on_device(): pl.pallas_call(owner_kernel, in_specs=[smem] + [vmem] * 5 + [far] * 12, o...  10.4 us
    all_to_all x1, waiting for transfers between devices, on_device(): lax.all_to_all(outgoing, 'ctx', split_axis=0, concat_axis=0, tiled=True)  10.2 us
    psum x1, blocking collectives, on_device(): mine = lax.psum(halves[:64] + halves[64:], 'tp')  7.14 us
    all_to_all x1, starting transfers between devices, on_device(): lax.all_to_all(spread, 'ctx', split_axis=0, concat_axis=0, tiled=True)  6.16 us
  transfers between devices with their start and end apart: 2, of which 2 were waited for; matrix products, arithmetic and copies ran while one was open for 1% of the time, Pallas kernels for 13%

profile of v6, /device:TPU:4, one launch (start us, length us, event | category | flops | bytes accessed | tf_op | source)
XLA Modules:
  0.0 120.6 jit_solution(5441401688135499450)
XLA Ops:
  0.6 2.2 %pack_rows.1 = bf16[128,8,128]{2,1,0:T(8,128)(2,1)} custom-call(bf16[3,128,256]{2,1,0:T(8,128)(2,1)} %streams_ref.3, bf16[128,256]{1,0:T(8,128)(2,1)} %cot_ref.3), custom_call_target="tpu_custom_call" | custom-call | tf_op jit(solution)/shard_map/pack_rows/pallas_call | solution.py:546
  2.8 20.6 %all-to-all-start = ((bf16[128,8,128]{2,1,0:T(8,128)(2,1)}), bf16[128,8,128]{2,1,0:T(8,128)(2,1)S(1)}, u32[]{:S(2)}, u32[]{:S(2)}) async-start(bf16[128,8,128]{2,1,0:T(8,128)(2,1)} %pack_rows.1), calls=%async_computation | async-start | bytes 524288 | tf_op jit(solution)/shard_map/all_to_all | solution.py:552
  23.4 13.0 %filter_net.1 = (bf16[16384,128]{1,0:T(8,128)(2,1)}, bf16[64,16384]{1,0:T(8,128)(2,1)}, bf16[64,16384]{1,0:T(8,128)(2,1)}, bf16[64,16384]{1,0:T(8,128)(2,1)}, f3...) custom-call(s32[1]{0:T(128)} %bitcast.rank_ref, bf16[128,16384]{1,0:T(8,128)(2,1)} %constant.25.clone.feat_ref, ...), custom_call_target="tpu_custom_call" | custom-call | tf_op jit(solution)/shard_map/filter_net/pallas_call | solution.py:559
  36.4 10.2 %all-to-all-done.recv_ref = bf16[128,8,128]{2,1,0:T(8,128)(2,1)S(1)} async-done(((bf16[128,8,128]{2,1,0:T(8,128)(2,1)}), bf16[128,8,128]{2,1,0:T(8,128)(2,1)S(1)}, u32[]{:S(2)}, u32[]{:S(2)}) %all-to-all-start) | async-done | bytes 262176 | tf_op jit(solution)/shard_map/all_to_all | solution.py:552
  46.6 0.0 copy-start
  46.6 0.7 copy-done
  47.3 10.4 %convolve_channels.1 = (bf16[128,2,384]{2,1,0:T(2,128)(2,1)}, f32[1,256]{1,0:T(1,128)}) custom-call(s32[1]{0:T(128)} %bitcast.rank_ref, f32[3,3,256]{2,1,0:T(4,128)} %taps_ref.3, f32[1,256]{1,0:T(1,128)} %bitcast.19, f32[1,256]{1,0:T(1,128)} %bitcast.18, f32[64,64]{1,0:T(8,128)} %w2_ref.3, f32[64,256]{1,0:T(8,128)} %wl_ref.3, bf16[128,8,128]{2,1,0:T(8,128)(2,1)} %copy-done, ...), custom_call_target="tpu_custom_call" | custom-call | tf_op jit(solution)/shard_map/convolve_channels/pallas_call | solution.py:610
  57.7 27.0 %all_to_all.15 = bf16[128,2,384]{2,1,0:T(2,128)(2,1)S(1)} all-to-all(bf16[128,2,384]{2,1,0:T(2,128)(2,1)} %get-tuple-element.36), channel_id=1, replica_groups=mesh['ctx'=128,'tp'=4] {'ctx'}, dimensions={0} | all-to-all | bytes 393216 | tf_op jit(solution)/shard_map/all_to_all | solution.py:635
  84.7 0.8 slice.15
  85.4 0.2 convert_reduce_fusion
  85.6 0.1 add_bitcast_fusion
  85.6 7.1 %psum.7 = f32[1,64]{1,0:T(1,128)S(1)} all-reduce(f32[1,64]{1,0:T(1,128)S(1)} %add_bitcast_fusion), channel_id=1, replica_groups=mesh['ctx'=128,'tp'=4] {'tp'}, use_global_device_ids=true, to_apply=%region_1.0 | all-reduce | flops 64 | bytes 512 | tf_op jit(solution)/shard_map/psum | solution.py:639
  92.8 0.1 pad_maximum_fusion
  92.9 0.7 broadcast_in_dim.30
  93.6 6.2 %all-to-all-start.2 = ((f32[128,1,256]{2,1,0:T(1,128)}), f32[128,1,256]{2,1,0:T(1,128)S(1)}, u32[]{:S(2)}, u32[]{:S(2)}) async-start(f32[128,1,256]{2,1,0:T(1,128)} %broadcast_in_dim.30), calls=%async_computation.2 | async-start | bytes 262144 | tf_op jit(solution)/shard_map/all_to_all | solution.py:642
  99.8 0.7 copy.26
  100.5 2.2 %finish_rows.1 = (bf16[128,256]{1,0:T(8,128)(2,1)}, bf16[3,128,256]{2,1,0:T(8,128)(2,1)}) custom-call(bf16[128,768]{1,0:T(8,128)(2,1)} %bitcast.15, bf16[3,128,256]{2,1,0:T(8,128)(2,1)} %streams_ref.3, bf16[128,256]{1,0:T(8,128)(2,1)} %cot_ref.3, f32[3,3,256]{2,1,0:T(4,128)} %taps_ref.3), custom_call_target="tpu_custom_call" | custom-call | tf_op jit(solution)/shard_map/finish_rows/pallas_call | solution.py:643
  102.6 15.5 %all-to-all-done.2.far_ref = f32[128,1,256]{2,1,0:T(1,128)S(1)} async-done(((f32[128,1,256]{2,1,0:T(1,128)}), f32[128,1,256]{2,1,0:T(1,128)S(1)}, u32[]{:S(2)}, u32[]{:S(2)}) %all-to-all-start.2) | async-done | bytes 131104 | tf_op jit(solution)/shard_map/all_to_all | solution.py:642
  118.1 0.0 copy-start.1
  118.1 0.7 copy-done.1
  118.7 1.7 %unpack_sums.1 = (f32[3,3,256]{2,1,0:T(4,128)}, f32[33,64]{1,0:T(8,128)}, f32[1,64]{1,0:T(1,128)}, f32[64,64]{1,0:T(8,128)}, f32[1,64]{1,0:T(1,128)}, /*index=5*...) custom-call(f32[128,1,256]{2,1,0:T(1,128)} %copy-done.1), custom_call_target="tpu_custom_call" | custom-call | tf_op jit(solution)/shard_map/unpack_sums/pallas_call | solution.py:649
Async XLA Ops:
  2.8 43.8 %all-to-all-start = ((bf16[128,8,128]{2,1,0:T(8,128)(2,1)}), bf16[128,8,128]{2,1,0:T(8,128)(2,1)S(1)}, u32[]{:S(2)}, u32[]{:S(2)}) async-start(bf16[128,8,128]{2,1,0:T(8,128)(2,1)} %pack_rows.1), calls=%async_computation | async-start | bytes 524288 | tf_op jit(solution)/shard_map/all_to_all | solution.py:552
  46.6 0.7 copy-start
  93.6 24.5 %all-to-all-start.2 = ((f32[128,1,256]{2,1,0:T(1,128)}), f32[128,1,256]{2,1,0:T(1,128)S(1)}, u32[]{:S(2)}, u32[]{:S(2)}) async-start(f32[128,1,256]{2,1,0:T(1,128)} %broadcast_in_dim.30), calls=%async_computation.2 | async-start | bytes 262144 | tf_op jit(solution)/shard_map/all_to_all | solution.py:642
  118.1 0.7 copy-start.1
